TPU v7x, 128 devices: a whole 4x4x4 slice. The times are simulated.
128 devices in a mesh: dev: 128 (over z, y, x, core).
Axes of the slice: x: 4, y: 4, z: 4, core: 2. Of those that a mesh axis runs over, the one named last changes fastest.
Arguments:
- emb: bfloat16 [131072, 768], P('dev')
- cluster: int32 [131072], P('dev'), may hold values from 0 to 1023, as said below
- rank: int32 [131072], P('dev'), may hold values from 0 to 262143, as said below
Outputs:
- nearest: float32 [131072], P('dev')
Inputs may be any that keep to these rules, and one draw needn't show every extreme that they name: Item i is placed on device (cluster[i] mod N + rank[i] mod 2) mod N of dev, N its number of devices (each cluster's items are split by rank parity over two neighbouring devices to bound the items any one device receives); the 1024 items of one device place at most 16 items on any one device, and exactly 16 on some device. `rank`: ranks are distinct over all items.
All inputs are finite; a program needn't handle non-finite values.
Results may differ from a plain program's by a relative error of at most 0.0005.
Values may be sent and summed in bfloat16 or wider, within the bound.
No kernel may reach another device: no remote copies, remote signals or barrier semaphores. Data moves between devices by JAX's collectives and lax.ppermute only.
A program may use at most 64 MiB of HBM per device.

v0:
```python
import jax
import jax.numpy as jnp
from jax import lax
from jax.sharding import PartitionSpec as P


def passed_along(array, axis, by):
    length = lax.axis_size(axis)
    return lax.ppermute(array, axis, [(i, (i + by) % length) for i in range(length)])


def paired_best(left, right):
    left_unit, left_cluster, left_rank = left
    right_unit, right_cluster, right_rank = right
    pool_rows, feature_width = left_unit.shape
    block_rows = min(512, pool_rows)
    block_count = pool_rows // block_rows
    blocked = (
        left_unit.reshape(block_count, block_rows, feature_width),
        left_cluster.reshape(block_count, block_rows),
        left_rank.reshape(block_count, block_rows),
    )

    def advance(column_best, pieces):
        piece_unit, piece_cluster, piece_rank = pieces
        similar = lax.dot_general(
            piece_unit, right_unit, (((1,), (1,)), ((), ())), preferred_element_type=jnp.float32
        )
        same_cluster = (piece_cluster[:, None] == right_cluster[None, :]) & (
            right_cluster[None, :] >= 0
        )
        row_best = jnp.max(
            jnp.where(same_cluster & (right_rank[None, :] < piece_rank[:, None]), similar, -1.0),
            axis=1,
        )
        return (column_best, row_best)

    start_value = jnp.full((right_unit.shape[0],), -1.0, jnp.float32)
    column_best, row_best = lax.scan(advance, start_value, blocked)
    return (row_best.reshape(-1), column_best)


def per_device(emb, cluster, rank):
    row_count, feature_width = emb.shape
    devices = lax.axis_size("dev")
    capacity = 2 * row_count // devices
    pool_rows = devices * capacity
    widened = emb.astype(jnp.float32)
    unit_rows = (
        widened * lax.rsqrt(jnp.sum(widened * widened, axis=-1, keepdims=True) + 1e-06)
    ).astype(jnp.bfloat16)
    target_dev = (cluster % devices + rank % 2) % devices
    one_hot = (target_dev[:, None] == jnp.arange(devices, dtype=jnp.int32)[None, :]).astype(
        jnp.int32
    )
    slot_index = jnp.sum(jnp.cumsum(one_hot, axis=0) * one_hot, axis=1) - 1
    placing = target_dev * capacity + slot_index
    send_unit = jnp.zeros((pool_rows, feature_width), jnp.bfloat16).at[placing].set(unit_rows)
    send_cluster = jnp.full((pool_rows,), -1, jnp.int32).at[placing].set(cluster)
    send_rank = jnp.zeros((pool_rows,), jnp.int32).at[placing].set(rank)
    received = (
        lax.all_to_all(send_unit, "dev", split_axis=0, concat_axis=0, tiled=True),
        lax.all_to_all(send_cluster, "dev", split_axis=0, concat_axis=0, tiled=True),
        lax.all_to_all(send_rank, "dev", split_axis=0, concat_axis=0, tiled=True),
    )
    inner_best, unused = paired_best(received, received)
    lower = passed_along((received[0], received[1], received[2]), "dev", 1)
    upper = passed_along((received[0], received[1], received[2]), "dev", -1)
    lower_best, unused_low = paired_best(received, lower)
    upper_best, unused_up = paired_best(received, upper)
    best_found = jnp.maximum(inner_best, jnp.maximum(lower_best, upper_best))
    back_home = lax.all_to_all(best_found, "dev", split_axis=0, concat_axis=0, tiled=True)
    return back_home[placing]


def solution(mesh):
    placed = (P("dev", None), P("dev"), P("dev"))
    return jax.shard_map(
        per_device, mesh=mesh, in_specs=placed, out_specs=P("dev"), check_vma=False
    )
```

profile of v0, /device:TPU:1, one launch (start us, length us, event | category | flops | bytes accessed | tf_op | source)
XLA Modules:
  0.0 203.9 jit_solution(4306233772499296139)
XLA Ops:
  0.0 0.8 add_select_fusion
  1.4 0.4 fusion.15
  1.7 4.5 %scatter_custom_fusion = s32[2048]{0:T(1024)S(1)} fusion(s32[1024]{0:T(1024)S(1)} %get-tuple-element.183, s32[1024]{0:T(1024)} %param.10, s32[]{:T(128)} %constant.95.clone.1), kind=kCustom, calls=%fused_computation.59 | custom fusion | bytes 8704 | tf_op jit(solution)/shard_map/scatter | solution.py:59
  6.2 0.7 all_to_all.30
  6.9 11.5 %all-to-all-start = ((s32[128,16,1]{1,2,0:T(1,128)}), s32[128,16,1]{1,2,0:T(1,128)S(1)}, u32[]{:S(2)}, u32[]{:S(2)}) async-start(s32[128,16,1]{1,2,0:T(1,128)} %bitcast.16), calls=%async_computation | async-start | bytes 131072 | tf_op jit(solution)/shard_map/all_to_all | solution.py:63
  18.4 0.4 fusion.9
  18.8 4.5 %scatter_custom_fusion.1 = s32[2048]{0:T(1024)S(1)} fusion(s32[1024]{0:T(1024)S(1)} %get-tuple-element.183, s32[1024]{0:T(1024)} %param.11, s32[]{:T(128)} %constant.87.clone.1), kind=kCustom, calls=%fused_computation.57 | custom fusion | bytes 8704 | tf_op jit(solution)/shard_map/scatter | solution.py:60
  23.3 0.7 all_to_all.33
  24.0 4.0 %all-to-all-done = s32[128,16,1]{1,2,0:T(1,128)S(1)} async-done(((s32[128,16,1]{1,2,0:T(1,128)}), s32[128,16,1]{1,2,0:T(1,128)S(1)}, u32[]{:S(2)}, u32[]{:S(2)}) %all-to-all-start) | async-done | bytes 8224 | tf_op jit(solution)/shard_map/all_to_all | solution.py:63
  28.0 5.7 %all-to-all-start.1 = ((s32[128,16,1]{1,2,0:T(1,128)}), s32[128,16,1]{1,2,0:T(1,128)S(1)}, u32[]{:S(2)}, u32[]{:S(2)}) async-start(s32[128,16,1]{1,2,0:T(1,128)} %bitcast.17), calls=%async_computation.1 | async-start | bytes 131072 | tf_op jit(solution)/shard_map/all_to_all | solution.py:64
  33.8 7.8 %scatter_custom_fusion.2 = bf16[2048,768]{1,0:T(8,128)(2,1)} fusion(s32[1024]{0:T(1024)S(1)} %get-tuple-element.183, bf16[1024,768]{1,0:T(8,128)(2,1)S(1)} %copy-done, f32[1024]{0:T(1024)S(1)} %add_rsqrt_fusion, bf16[]{:T(256)} %constant.89.clone.1), kind=kCustom, calls=%fused_computation.29 | custom fusion | flops 2359296 | bytes 4722690 | tf_op jit(solution)/shard_map/scatter | solution.py:58
  41.5 1.8 all-to-all-done.1
  43.4 8.3 %all-to-all-start.2 = ((bf16[128,16,768]{2,1,0:T(8,128)(2,1)}), bf16[128,16,768]{2,1,0:T(8,128)(2,1)}, u32[]{:S(2)}, u32[]{:S(2)}) async-start(bf16[128,16,768]{2,1,0:T(8,128)(2,1)} %bitcast.18), calls=%async_computation.2 | async-start | bytes 6291456 | tf_op jit(solution)/shard_map/all_to_all | solution.py:62
  51.7 0.7 all_to_all.32
  52.4 1.6 collective-permute-start
  54.0 0.5 broadcast.104
  54.5 0.7 reduce.14
  55.3 0.7 all_to_all.35
  56.0 1.7 collective-permute-start.1
  57.7 4.9 %collective-permute-start.4 = (s32[2048]{0:T(1024)}, s32[2048]{0:T(1024)S(1)}, u32[]{:S(2)}, u32[]{:S(2)}) collective-permute-start(s32[2048]{0:T(1024)} %all_to_all.35), channel_id=1, source_target_pairs={{0,127},{1,0},{2,1},{3,2},{4,3},{5,4},{6,5},{7,6},{8,7},{9,8},{10,... | collective-permute-start | bytes 24584 | tf_op jit(solution)/shard_map/ppermute | solution.py:9
  62.6 0.7 reduce.13
  63.6 29.7 %all-to-all-done.2 = bf16[128,16,768]{2,1,0:T(8,128)(2,1)} async-done(((bf16[128,16,768]{2,1,0:T(8,128)(2,1)}), bf16[128,16,768]{2,1,0:T(8,128)(2,1)}, u32[]{:S(2)}, u32[]{:S(2)}) %all-to-all-start.2) | async-done | bytes 3145760 | tf_op jit(solution)/shard_map/all_to_all | solution.py:62
  93.2 1.1 collective-permute-start.2
  94.3 20.0 %while.30 = (s32[]{:T(128)}, f32[4,512]{1,0:T(4,128)S(1)}, s32[4,512]{1,0:T(4,128)S(1)}, s32[2048]{0:T(1024)}, s32[2048]{0:T(1024)}, /*index=5*/s32[4,512]{1,0:T...) while((s32[]{:T(128)}, f32[4,512]{1,0:T(4,128)S(1)}, ...), condition=%wide.region_9.10_spmd, body=%wide.region_7.9_spmd.sunk | while | flops 1616905728 | bytes 3979385 | solution.py:39
  94.3 0.7 broadcast_compare_fusion.6
  95.0 4.2 %select_reduce_fusion.6 = f32[512]{0:T(512)S(1)} fusion(bf16[2048,768]{1,0:T(8,128)(2,1)} %get-tuple-element.376, s32[2048]{0:T(1024)} %get-tuple-element.373, s32[2048]{0:T(1024)} %get-tuple-element.372, s32[512]{0:T(512)S(1)} %bitcast.75, s32[512]{0:T(512)S(1)} %bitcast.76, pred[2048]{0:T(1024)(128)(4,1)S(1)} %broadcast_compare_fusion.6, ...), kind=kOutput, calls=%fused_computation.4.clone.1 | convolution fusion | flops 1616903680 | bytes 3956740 | tf_op jit(solution)/shard_map/while/body/eval_jaxpr/dot_general | solution.py:26
  99.3 0.7 broadcast_compare_fusion.6
  100.0 4.2 %select_reduce_fusion.6 = f32[512]{0:T(512)S(1)} fusion(bf16[2048,768]{1,0:T(8,128)(2,1)} %get-tuple-element.376, s32[2048]{0:T(1024)} %get-tuple-element.373, s32[2048]{0:T(1024)} %get-tuple-element.372, s32[512]{0:T(512)S(1)} %bitcast.75, s32[512]{0:T(512)S(1)} %bitcast.76, pred[2048]{0:T(1024)(128)(4,1)S(1)} %broadcast_compare_fusion.6, ...), kind=kOutput, calls=%fused_computation.4.clone.1 | convolution fusion | flops 1616903680 | bytes 3956740 | tf_op jit(solution)/shard_map/while/body/eval_jaxpr/dot_general | solution.py:26
  104.3 0.7 broadcast_compare_fusion.6
  105.0 4.2 %select_reduce_fusion.6 = f32[512]{0:T(512)S(1)} fusion(bf16[2048,768]{1,0:T(8,128)(2,1)} %get-tuple-element.376, s32[2048]{0:T(1024)} %get-tuple-element.373, s32[2048]{0:T(1024)} %get-tuple-element.372, s32[512]{0:T(512)S(1)} %bitcast.75, s32[512]{0:T(512)S(1)} %bitcast.76, pred[2048]{0:T(1024)(128)(4,1)S(1)} %broadcast_compare_fusion.6, ...), kind=kOutput, calls=%fused_computation.4.clone.1 | convolution fusion | flops 1616903680 | bytes 3956740 | tf_op jit(solution)/shard_map/while/body/eval_jaxpr/dot_general | solution.py:26
  109.3 0.7 broadcast_compare_fusion.6
  110.0 4.2 %select_reduce_fusion.6 = f32[512]{0:T(512)S(1)} fusion(bf16[2048,768]{1,0:T(8,128)(2,1)} %get-tuple-element.376, s32[2048]{0:T(1024)} %get-tuple-element.373, s32[2048]{0:T(1024)} %get-tuple-element.372, s32[512]{0:T(512)S(1)} %bitcast.75, s32[512]{0:T(512)S(1)} %bitcast.76, pred[2048]{0:T(1024)(128)(4,1)S(1)} %broadcast_compare_fusion.6, ...), kind=kOutput, calls=%fused_computation.4.clone.1 | convolution fusion | flops 1616903680 | bytes 3956740 | tf_op jit(solution)/shard_map/while/body/eval_jaxpr/dot_general | solution.py:26
  114.4 14.4 %collective-permute-done.2 = bf16[2048,768]{1,0:T(8,128)(2,1)} collective-permute-done((bf16[2048,768]{1,0:T(8,128)(2,1)}, bf16[2048,768]{1,0:T(8,128)(2,1)}, u32[]{:S(2)}, u32[]{:S(2)}) %collective-permute-start.2) | collective-permute-done | bytes 3145760 | tf_op jit(solution)/shard_map/ppermute | solution.py:9
  128.8 17.6 %while.31 = (s32[]{:T(128)}, f32[4,512]{1,0:T(4,128)S(1)}, s32[4,512]{1,0:T(4,128)S(1)}, s32[2048]{0:T(1024)S(1)}, s32[2048]{0:T(1024)S(1)}, /*index=5*/s32[4,51...) while((s32[]{:T(128)}, f32[4,512]{1,0:T(4,128)S(1)}, ...), condition=%wide.region_12.13_spmd, body=%wide.region_10.12_spmd.sunk | while | flops 1616905728 | bytes 3979385 | solution.py:39
  128.8 4.3 %select_reduce_fusion.7 = f32[512]{0:T(512)S(1)} fusion(bf16[2048,768]{1,0:T(8,128)(2,1)} %get-tuple-element.406, s32[2048]{0:T(1024)S(1)} %get-tuple-element.403, s32[2048]{0:T(1024)S(1)} %get-tuple-element.402, s32[512]{0:T(512)S(1)} %bitcast.77, s32[512]{0:T(512)S(1)} %bitcast.78, pred[2048]{0:T(1024)(128)(4,1)S(1)} %broadcast_compare_fusion.7, ...), kind=kOutput, calls=%fused_computation.11.clone.1 | convolution fusion | flops 1616903680 | bytes 3956740 | tf_op jit(solution)/shard_map/while/body/eval_jaxpr/dot_general | solution.py:26
  133.2 4.3 %select_reduce_fusion.7 = f32[512]{0:T(512)S(1)} fusion(bf16[2048,768]{1,0:T(8,128)(2,1)} %get-tuple-element.406, s32[2048]{0:T(1024)S(1)} %get-tuple-element.403, s32[2048]{0:T(1024)S(1)} %get-tuple-element.402, s32[512]{0:T(512)S(1)} %bitcast.77, s32[512]{0:T(512)S(1)} %bitcast.78, pred[2048]{0:T(1024)(128)(4,1)S(1)} %broadcast_compare_fusion.7, ...), kind=kOutput, calls=%fused_computation.11.clone.1 | convolution fusion | flops 1616903680 | bytes 3956740 | tf_op jit(solution)/shard_map/while/body/eval_jaxpr/dot_general | solution.py:26
  137.6 4.3 %select_reduce_fusion.7 = f32[512]{0:T(512)S(1)} fusion(bf16[2048,768]{1,0:T(8,128)(2,1)} %get-tuple-element.406, s32[2048]{0:T(1024)S(1)} %get-tuple-element.403, s32[2048]{0:T(1024)S(1)} %get-tuple-element.402, s32[512]{0:T(512)S(1)} %bitcast.77, s32[512]{0:T(512)S(1)} %bitcast.78, pred[2048]{0:T(1024)(128)(4,1)S(1)} %broadcast_compare_fusion.7, ...), kind=kOutput, calls=%fused_computation.11.clone.1 | convolution fusion | flops 1616903680 | bytes 3956740 | tf_op jit(solution)/shard_map/while/body/eval_jaxpr/dot_general | solution.py:26
  142.0 4.3 %select_reduce_fusion.7 = f32[512]{0:T(512)S(1)} fusion(bf16[2048,768]{1,0:T(8,128)(2,1)} %get-tuple-element.406, s32[2048]{0:T(1024)S(1)} %get-tuple-element.403, s32[2048]{0:T(1024)S(1)} %get-tuple-element.402, s32[512]{0:T(512)S(1)} %bitcast.77, s32[512]{0:T(512)S(1)} %bitcast.78, pred[2048]{0:T(1024)(128)(4,1)S(1)} %broadcast_compare_fusion.7, ...), kind=kOutput, calls=%fused_computation.11.clone.1 | convolution fusion | flops 1616903680 | bytes 3956740 | tf_op jit(solution)/shard_map/while/body/eval_jaxpr/dot_general | solution.py:26
  146.4 5.0 %collective-permute-done.5 = bf16[2048,768]{1,0:T(8,128)(2,1)} collective-permute-done((bf16[2048,768]{1,0:T(8,128)(2,1)}, bf16[2048,768]{1,0:T(8,128)(2,1)}, u32[]{:S(2)}, u32[]{:S(2)}) %collective-permute-start.5) | collective-permute-done | bytes 3145760 | tf_op jit(solution)/shard_map/ppermute | solution.py:9
  151.4 17.5 %while.32 = (s32[]{:T(128)}, f32[4,512]{1,0:T(4,128)S(1)}, s32[4,512]{1,0:T(4,128)S(1)}, s32[2048]{0:T(1024)S(1)}, s32[2048]{0:T(1024)S(1)}, /*index=5*/s32[4,51...) while((s32[]{:T(128)}, f32[4,512]{1,0:T(4,128)S(1)}, ...), condition=%wide.region_15.16_spmd, body=%wide.region_13.15_spmd.sunk | while | flops 1616905728 | bytes 3979385 | solution.py:39
  151.4 4.3 %select_reduce_fusion.8 = f32[512]{0:T(512)S(1)} fusion(bf16[2048,768]{1,0:T(8,128)(2,1)} %get-tuple-element.436, s32[2048]{0:T(1024)S(1)} %get-tuple-element.433, s32[2048]{0:T(1024)S(1)} %get-tuple-element.432, s32[512]{0:T(512)S(1)} %bitcast.79, s32[512]{0:T(512)S(1)} %bitcast.80, pred[2048]{0:T(1024)(128)(4,1)S(1)} %broadcast_compare_fusion.8, ...), kind=kOutput, calls=%fused_computation.18.clone.1 | convolution fusion | flops 1616903680 | bytes 3956740 | tf_op jit(solution)/shard_map/while/body/eval_jaxpr/dot_general | solution.py:26
  155.8 4.3 %select_reduce_fusion.8 = f32[512]{0:T(512)S(1)} fusion(bf16[2048,768]{1,0:T(8,128)(2,1)} %get-tuple-element.436, s32[2048]{0:T(1024)S(1)} %get-tuple-element.433, s32[2048]{0:T(1024)S(1)} %get-tuple-element.432, s32[512]{0:T(512)S(1)} %bitcast.79, s32[512]{0:T(512)S(1)} %bitcast.80, pred[2048]{0:T(1024)(128)(4,1)S(1)} %broadcast_compare_fusion.8, ...), kind=kOutput, calls=%fused_computation.18.clone.1 | convolution fusion | flops 1616903680 | bytes 3956740 | tf_op jit(solution)/shard_map/while/body/eval_jaxpr/dot_general | solution.py:26
  160.2 4.3 %select_reduce_fusion.8 = f32[512]{0:T(512)S(1)} fusion(bf16[2048,768]{1,0:T(8,128)(2,1)} %get-tuple-element.436, s32[2048]{0:T(1024)S(1)} %get-tuple-element.433, s32[2048]{0:T(1024)S(1)} %get-tuple-element.432, s32[512]{0:T(512)S(1)} %bitcast.79, s32[512]{0:T(512)S(1)} %bitcast.80, pred[2048]{0:T(1024)(128)(4,1)S(1)} %broadcast_compare_fusion.8, ...), kind=kOutput, calls=%fused_computation.18.clone.1 | convolution fusion | flops 1616903680 | bytes 3956740 | tf_op jit(solution)/shard_map/while/body/eval_jaxpr/dot_general | solution.py:26
  164.6 4.3 %select_reduce_fusion.8 = f32[512]{0:T(512)S(1)} fusion(bf16[2048,768]{1,0:T(8,128)(2,1)} %get-tuple-element.436, s32[2048]{0:T(1024)S(1)} %get-tuple-element.433, s32[2048]{0:T(1024)S(1)} %get-tuple-element.432, s32[512]{0:T(512)S(1)} %bitcast.79, s32[512]{0:T(512)S(1)} %bitcast.80, pred[2048]{0:T(1024)(128)(4,1)S(1)} %broadcast_compare_fusion.8, ...), kind=kOutput, calls=%fused_computation.18.clone.1 | convolution fusion | flops 1616903680 | bytes 3956740 | tf_op jit(solution)/shard_map/while/body/eval_jaxpr/dot_general | solution.py:26
  169.1 22.9 %all_to_all.45 = f32[128,16,1]{1,2,0:T(1,128)S(1)} all-to-all(f32[128,16,1]{1,2,0:T(1,128)S(1)} %bitcast.73), channel_id=1, replica_groups=mesh['dev'=128] {'dev'}, dimensions={0} | all-to-all | bytes 16384 | tf_op jit(solution)/shard_map/all_to_all | solution.py:72
  191.9 0.5 broadcast.106
  192.4 0.8 reduce.15
  193.3 10.5 %gather_fusion = f32[1024]{0:T(1024)} fusion(f32[2048]{0:T(1024)S(1)} %all_to_all.40, s32[1024]{0:T(1024)S(1)} %get-tuple-element.182), kind=kCustom, calls=%fused_computation | custom fusion | bytes 12288 | tf_op jit(solution)/shard_map/gather | solution.py:73
  (57 shorter events, 1.7 us)
Async XLA Ops:
  0.0 18.4 %copy-start = (bf16[1024,768]{1,0:T(8,128)(2,1)S(1)}, bf16[1024,768]{1,0:T(8,128)(2,1)}, u32[]{:S(2)}) copy-start(bf16[1024,768]{1,0:T(8,128)(2,1)} %param.9) | copy-start | bytes 4718596
  6.9 21.1 %all-to-all-start = ((s32[128,16,1]{1,2,0:T(1,128)}), s32[128,16,1]{1,2,0:T(1,128)S(1)}, u32[]{:S(2)}, u32[]{:S(2)}) async-start(s32[128,16,1]{1,2,0:T(1,128)} %bitcast.16), calls=%async_computation | async-start | bytes 131072 | tf_op jit(solution)/shard_map/all_to_all | solution.py:63
  28.0 15.3 %all-to-all-start.1 = ((s32[128,16,1]{1,2,0:T(1,128)}), s32[128,16,1]{1,2,0:T(1,128)S(1)}, u32[]{:S(2)}, u32[]{:S(2)}) async-start(s32[128,16,1]{1,2,0:T(1,128)} %bitcast.17), calls=%async_computation.1 | async-start | bytes 131072 | tf_op jit(solution)/shard_map/all_to_all | solution.py:64
  43.4 49.9 %all-to-all-start.2 = ((bf16[128,16,768]{2,1,0:T(8,128)(2,1)}), bf16[128,16,768]{2,1,0:T(8,128)(2,1)}, u32[]{:S(2)}, u32[]{:S(2)}) async-start(bf16[128,16,768]{2,1,0:T(8,128)(2,1)} %bitcast.18), calls=%async_computation.2 | async-start | bytes 6291456 | tf_op jit(solution)/shard_map/all_to_all | solution.py:62
  52.4 61.9 %collective-permute-start = (s32[2048]{0:T(1024)}, s32[2048]{0:T(1024)S(1)}, u32[]{:S(2)}, u32[]{:S(2)}) collective-permute-start(s32[2048]{0:T(1024)} %all_to_all.32), channel_id=1, source_target_pairs={{0,1},{1,2},{2,3},{3,4},{4,5},{5,6},{6,7},{7,8},{8,9},{9,10},{10,1... | collective-permute-start | bytes 24584 | tf_op jit(solution)/shard_map/ppermute | solution.py:9
  54.0 92.4 %collective-permute-start.3 = (s32[2048]{0:T(1024)}, s32[2048]{0:T(1024)S(1)}, u32[]{:S(2)}, u32[]{:S(2)}) collective-permute-start(s32[2048]{0:T(1024)} %all_to_all.32), channel_id=1, source_target_pairs={{0,127},{1,0},{2,1},{3,2},{4,3},{5,4},{6,5},{7,6},{8,7},{9,8},{10,... | collective-permute-start | bytes 24584 | tf_op jit(solution)/shard_map/ppermute | solution.py:9
  56.0 58.5 %collective-permute-start.1 = (s32[2048]{0:T(1024)}, s32[2048]{0:T(1024)S(1)}, u32[]{:S(2)}, u32[]{:S(2)}) collective-permute-start(s32[2048]{0:T(1024)} %all_to_all.35), channel_id=1, source_target_pairs={{0,1},{1,2},{2,3},{3,4},{4,5},{5,6},{6,7},{7,8},{8,9},{9,10},{10,1... | collective-permute-start | bytes 24584 | tf_op jit(solution)/shard_map/ppermute | solution.py:9
  57.7 88.7 %collective-permute-start.4 = (s32[2048]{0:T(1024)}, s32[2048]{0:T(1024)S(1)}, u32[]{:S(2)}, u32[]{:S(2)}) collective-permute-start(s32[2048]{0:T(1024)} %all_to_all.35), channel_id=1, source_target_pairs={{0,127},{1,0},{2,1},{3,2},{4,3},{5,4},{6,5},{7,6},{8,7},{9,8},{10,... | collective-permute-start | bytes 24584 | tf_op jit(solution)/shard_map/ppermute | solution.py:9
  93.2 35.6 %collective-permute-start.2 = (bf16[2048,768]{1,0:T(8,128)(2,1)}, bf16[2048,768]{1,0:T(8,128)(2,1)}, u32[]{:S(2)}, u32[]{:S(2)}) collective-permute-start(bf16[2048,768]{1,0:T(8,128)(2,1)} %bitcast.20), channel_id=1, source_target_pairs={{0,1},{1,2},{2,3},{3,4},{4,5},{5,6},{6,7},{7,8},{8,9},{9,10},{10,1... | collective-permute-start | bytes 9437192 | tf_op jit(solution)/shard_map/ppermute | solution.py:9
  114.3 37.1 %collective-permute-start.5 = (bf16[2048,768]{1,0:T(8,128)(2,1)}, bf16[2048,768]{1,0:T(8,128)(2,1)}, u32[]{:S(2)}, u32[]{:S(2)}) collective-permute-start(bf16[2048,768]{1,0:T(8,128)(2,1)} %bitcast.20), channel_id=1, source_target_pairs={{0,127},{1,0},{2,1},{3,2},{4,3},{5,4},{6,5},{7,6},{8,7},{9,8},{10,... | collective-permute-start | bytes 9437192 | tf_op jit(solution)/shard_map/ppermute | solution.py:9
where the time goes:
time: 204 us
  waiting for transfers between devices  54.9 us (27%)
  matrix products  51.2 us (25%)
  starting transfers between devices  35 us (17%)
  local copies, waits for them, and re-layouts  24.6 us (12%)
  blocking collectives  22.9 us (11%)
  other arithmetic  14.7 us (7%)
    dot_general x12, matrix products, advance(): lax.dot_general(piece_unit, right_unit, (((1,), (1,)), ((), ())), preferr...  51.2 us
    all_to_all x1, waiting for transfers between devices, per_device(): lax.all_to_all(send_unit, 'dev', split_axis=0, concat_axis=0, tiled=True)  29.7 us
    all_to_all x1, blocking collectives, per_device(): lax.all_to_all(best_found, 'dev', split_axis=0, concat_axis=0, tiled=True)  22.9 us
    ppermute x6, waiting for transfers between devices, passed_along(): lax.ppermute(array, axis, [(i, (i + by) % length) for i in range(length)])  19.4 us
    all_to_all x1, starting transfers between devices, per_device(): lax.all_to_all(send_cluster, 'dev', split_axis=0, concat_axis=0, tiled=True)  11.5 us
    gather x1, local copies, waits for them, and re-layouts, per_device(): return back_home[placing]  10.5 us
    ppermute x6, starting transfers between devices, passed_along(): lax.ppermute(array, axis, [(i, (i + by) % length) for i in range(length)])  9.44 us
    all_to_all x1, starting transfers between devices, per_device(): lax.all_to_all(send_unit, 'dev', split_axis=0, concat_axis=0, tiled=True)  8.33 us
  transfers between devices with their start and end apart: 9, of which 5 were waited for; matrix products, arithmetic and copies ran while one was open for 26% of the time, Pallas kernels for 0%

commit v1 on v0

v1 whole, which is shorter than its diff:
```python
import functools

import jax
import jax.numpy as jnp
from jax import lax
from jax.experimental import pallas as pl
from jax.experimental.pallas import tpu as pltpu
from jax.sharding import PartitionSpec as P

F32 = jnp.float32
BF16 = jnp.bfloat16
I32 = jnp.int32

N = 128
ROWS = 1024
D = 768
SLOTS = 10
MAIN = 8 * N
EXTRA = 2 * N
ALL = MAIN + EXTRA
NEAR = 176
FAR = 16
MOVED = 256
META = 128
HIGHEST = lax.Precision.HIGHEST
LIMIT = pltpu.CompilerParams(vmem_limit_bytes=56 * 1024 * 1024)


def iota(shape, dim):
    return lax.broadcasted_iota(I32, shape, dim)


def flag(mask, dtype=BF16):
    return jnp.where(mask, 1.0, 0.0).astype(dtype)


def dot(a, b, precision=None):
    return jnp.dot(a, b, preferred_element_type=F32, precision=precision)


def dot_nt(a, b, precision=None):
    return lax.dot_general(
        a, b, (((1,), (1,)), ((), ())), preferred_element_type=F32, precision=precision
    )


def pack_kernel(emb_ref, cluster_ref, rank_ref, out_ref, place_ref, unit, left, right):
    cluster = cluster_ref[...]
    rank = rank_ref[...]
    home = cluster % N
    member = cluster // N

    which = iota((N, ROWS), 0)
    at_home = which == home
    at_home_b = flag(at_home)
    chunks = jnp.concatenate([at_home_b[:, c * 128 : (c + 1) * 128] for c in range(8)], axis=0)
    lower = flag(iota((128, 128), 0) <= iota((128, 128), 1))
    running = dot(chunks, jnp.concatenate([lower, jnp.ones((128, 128), BF16)], axis=1))
    before = jnp.zeros((128, 128), F32)
    turn = []
    for c in range(8):
        part = running[c * 128 : (c + 1) * 128]
        turn.append(
            jnp.sum(
                jnp.where(at_home[:, c * 128 : (c + 1) * 128], part[:, :128] + before, 0.0),
                axis=0,
                keepdims=True,
            )
        )
        before = before + part[:, 128:]
    turn = jnp.concatenate(turn, axis=1) - 1.0

    count = dot_nt(jnp.ones((8, ROWS), BF16), at_home_b)
    window = count - float(SLOTS)
    queue = jnp.maximum(window, 0.0)
    for step in (1, 2, 4, 8, 16, 32, 64):
        queue = jnp.maximum(queue, window + pltpu.roll(queue, step, 1))
        window = window + pltpu.roll(window, step, 1)
    ahead = dot(pltpu.roll(queue, 1, 1), flag(at_home, F32), HIGHEST)[:1]
    offset = ahead + turn
    hops = jnp.floor((offset + 0.5) * (1.0 / SLOTS))
    slot = (offset - hops * SLOTS).astype(I32)
    hops = hops.astype(I32)
    target = (home + hops) % N
    place_ref[0:1, :] = home
    place_ref[1:2, :] = jnp.minimum(hops, 7) * 16 + slot

    for c in range(8):
        wide = emb_ref[c * 128 : (c + 1) * 128, :].astype(F32)
        scale = lax.rsqrt(jnp.sum(wide * wide, axis=-1, keepdims=True) + 1e-06)
        unit[c * 128 : (c + 1) * 128, :] = (wide * scale).astype(BF16)

    field = iota((META, ROWS), 0) // 16
    value = jnp.where(field == 0, member + 1, hops)
    value = jnp.where(field == 2, rank % 256, value)
    value = jnp.where(field == 3, (rank // 256) % 256, value)
    value = jnp.where(field == 4, rank // 65536, value)
    value = jnp.where((iota((META, ROWS), 0) % 16 == slot) & (field < 5), value, 0)
    meta = dot_nt(flag(which == target), value.astype(F32).astype(BF16))
    left[pl.ds(6, N, stride=8), :] = meta
    right[pl.ds(6, N, stride=8), :] = jnp.broadcast_to(jnp.minimum(queue[:1], 255.0), (N, 128))
    left[pl.ds(7, N, stride=8), :] = jnp.zeros((N, 128), F32)
    right[pl.ds(7, N, stride=8), :] = jnp.zeros((N, 128), F32)
    extra_row = jnp.where(slot >= 8, (slot - 8) * N + target, -1)
    late = dot(flag(iota((EXTRA, ROWS), 0) == extra_row), unit[...])
    for k in range(2):
        for piece in range(3):
            rows = late[k * N : (k + 1) * N, piece * 256 : (piece + 1) * 256]
            left[pl.ds(2 * piece + k, N, stride=8), :] = rows[:, :128]
            right[pl.ds(2 * piece + k, N, stride=8), :] = rows[:, 128:]
    out_ref[:, D : D + 128] = left[...].astype(BF16)
    out_ref[:, D + 128 :] = right[...].astype(BF16)

    main_row = jnp.where(slot < 8, target * 8 + slot, -1)
    for b in range(4):
        chosen = flag(iota((256, ROWS), 0) + b * 256 == main_row)
        out_ref[b * 256 : (b + 1) * 256, :D] = dot(chosen, unit[...]).astype(BF16)


def pack(emb, cluster, rank):
    return pl.pallas_call(
        pack_kernel,
        out_shape=(
            jax.ShapeDtypeStruct((MAIN, D + 256), BF16),
            jax.ShapeDtypeStruct((2, ROWS), I32),
        ),
        scratch_shapes=[
            pltpu.VMEM((ROWS, D), BF16),
            pltpu.VMEM((MAIN, 128), F32),
            pltpu.VMEM((MAIN, 128), F32),
        ],
        compiler_params=LIMIT,
        name="pack",
    )(emb, cluster.reshape(1, ROWS), rank.reshape(1, ROWS))


def unpack_kernel(
    got_ref, late_ref, column_ref, row_ref, near_ref, far_ref, bad_ref, left, right
):
    left[...] = got_ref[:, D : D + 128].astype(F32)
    right[...] = got_ref[:, D + 128 :].astype(F32)
    for k in range(2):
        for piece in range(3):
            for half, ref in enumerate((left, right)):
                at = piece * 256 + half * 128
                late_ref[k * N : (k + 1) * N, at : at + 128] = ref[
                    pl.ds(2 * piece + k, N, stride=8), :
                ].astype(BF16)
    meta = left[pl.ds(6, N, stride=8), :]
    queue = right[pl.ds(6, N, stride=8), :]
    meta_b = meta.astype(BF16)

    over_near = jnp.sum(jnp.minimum(queue, float(SLOTS)), axis=0, keepdims=True) - NEAR
    over_far = (
        jnp.sum(jnp.clip(queue - SLOTS, 0.0, float(SLOTS)), axis=0, keepdims=True) - FAR
    )
    over_long = jnp.max(queue, axis=0, keepdims=True) - 2.0 * SLOTS
    bad_ref[0, 0] = (
        jnp.max(jnp.maximum(jnp.maximum(over_near, over_far), over_long)) > 0.0
    ).astype(I32)

    spread = dot(flag(iota((MAIN, N), 0) // 8 == iota((MAIN, N), 1)), meta_b)
    spread = jnp.where(iota((MAIN, N), 1) % 16 == iota((MAIN, N), 0) % 8, spread, 0.0)
    lane = iota((N, N), 1)
    own = jnp.concatenate(
        [spread, jnp.where(lane % 16 == 8, meta, 0.0), jnp.where(lane % 16 == 9, meta, 0.0)],
        axis=0,
    ).astype(BF16)

    def weights(rows, shape, dim):
        field = iota(shape, dim) // 16
        weight = jnp.zeros(shape, F32)
        for at, by in rows:
            weight = jnp.where(field == at, by, weight)
        return weight.astype(BF16)

    rank_weights = ((2, 1.0), (3, 256.0), (4, 65536.0))
    cluster_weights = ((0, 1.0), (1, -16.0))
    column_ref[...] = dot(
        own,
        jnp.concatenate(
            [weights(rank_weights, (N, N), 0), weights(cluster_weights, (N, N), 0)], axis=1
        ),
    )
    row_ref[0:8, :] = dot_nt(weights(rank_weights, (8, N), 1), own)
    row_ref[8:16, :] = dot_nt(weights(cluster_weights, (8, N), 1), own)

    hops = pltpu.roll(meta, N - 16, 1)
    lower = flag(iota((N, N), 0) <= iota((N, N), 1))
    earlier = flag(iota((N, N), 0) > iota((N, N), 1))
    ones = jnp.ones((N, N), BF16)
    slot_of = iota((N, ALL), 1)
    slot_of = jnp.where(slot_of < MAIN, slot_of % 8, 8 + (slot_of - MAIN) // N)
    pick = flag(iota((N, ALL), 0) == slot_of)
    source_of = iota((N, ALL), 1)
    source_of = jnp.where(source_of < MAIN, source_of // 8, (source_of - MAIN) % N)
    of_source = iota((N, ALL), 0) == source_of

    field_lane = iota((N, N), 1)
    into = jnp.zeros((N, N), F32)
    for field, at in ((0, 2), (2, 3), (3, 4), (4, 5)):
        into = jnp.where((iota((N, N), 0) // 16 == field) & (field_lane == at), 1.0, into)
    card = dot(own, into.astype(BF16))
    line = iota((ALL, N), 0)
    card_lane = iota((ALL, N), 1)
    card = jnp.where(
        card_lane == 0, jnp.where(line < MAIN, line // 8, (line - MAIN) % N).astype(F32), card
    )
    card = jnp.where(
        card_lane == 1, jnp.where(line < MAIN, line % 8, 8 + (line - MAIN) // N).astype(F32), card
    )
    card = card.astype(BF16)

    for far, ref, length in ((1, near_ref, NEAR), (2, far_ref, FAR)):
        moves = (lane < SLOTS) & (meta > 0.0) & (hops == float(far))
        moves_b = flag(moves)
        number = dot(moves_b, lower) + dot(earlier, dot(moves_b, ones).astype(BF16))
        number = jnp.where(moves, number, 0.0).astype(BF16)
        number = jnp.sum(jnp.where(of_source, dot(number, pick), 0.0), axis=0, keepdims=True)
        chosen = flag(iota((length, ALL), 0) + 1 == number.astype(I32))
        sent = dot(chosen[:, :MAIN], got_ref[:, :D]) + dot(chosen[:, MAIN:], late_ref[...])
        ref[:, :D] = sent.astype(BF16)
        ref[:, D:] = dot(chosen, card).astype(BF16)


def unpack(got):
    return pl.pallas_call(
        unpack_kernel,
        out_shape=(
            jax.ShapeDtypeStruct((EXTRA, D), BF16),
            jax.ShapeDtypeStruct((ALL, 256), F32),
            jax.ShapeDtypeStruct((16, ALL), F32),
            jax.ShapeDtypeStruct((NEAR, D + META), BF16),
            jax.ShapeDtypeStruct((FAR, D + META), BF16),
            jax.ShapeDtypeStruct((1, 1), I32),
        ),
        out_specs=(pl.BlockSpec(memory_space=pltpu.VMEM),) * 5
        + (pl.BlockSpec(memory_space=pltpu.SMEM),),
        scratch_shapes=[pltpu.VMEM((MAIN, 128), F32), pltpu.VMEM((MAIN, 128), F32)],
        compiler_params=LIMIT,
        name="unpack",
    )(got)


def local_kernel(got_ref, late_ref, column_ref, row_ref, best_ref):
    best_ref[...] = jnp.full((8, ALL), -1.0, F32)

    def rows_of(b):
        if b * 256 < MAIN:
            return got_ref[b * 256 : (b + 1) * 256, :D]
        return late_ref[...]

    blocks = ALL // 256
    for i in range(blocks):
        rank = column_ref[i * 256 : (i + 1) * 256, :128]
        cluster = column_ref[i * 256 : (i + 1) * 256, 128:]
        rank = jnp.concatenate([rank, rank], axis=1)
        cluster = jnp.concatenate([cluster, cluster], axis=1)
        for j in range(blocks):
            across = slice(j * 256, (j + 1) * 256)
            similar = dot_nt(rows_of(i), rows_of(j))
            earlier = (cluster == row_ref[8:9, across]) & (rank < row_ref[0:1, across])
            kept = jnp.where(earlier, similar, -1.0)
            best_ref[:, across] = jnp.maximum(
                best_ref[:, across], jnp.max(kept.reshape(32, 8, 256), axis=0)
            )


def local_best(got, late, column, row):
    return pl.pallas_call(
        local_kernel,
        out_shape=jax.ShapeDtypeStruct((8, ALL), F32),
        compiler_params=LIMIT,
        cost_estimate=pl.CostEstimate(
            flops=2 * ALL * ALL * D, bytes_accessed=4 * ALL * D, transcendentals=0
        ),
        name="local_best",
    )(got, late, column, row)


def cross_kernel(got_ref, late_ref, row_ref, best_ref, near_ref, far_ref, out_ref, moved):
    moved[0:NEAR, :] = near_ref[...]
    moved[NEAR : NEAR + FAR, :] = far_ref[...]
    moved[NEAR + FAR :, :] = jnp.zeros((MOVED - NEAR - FAR, D + META), BF16)
    card = moved[:, D:]

    def weigh(rows, shape, dim):
        at = iota(shape, dim)
        weight = jnp.zeros(shape, F32)
        for lane, by in rows:
            weight = jnp.where(at == lane, by, weight)
        return weight.astype(BF16)

    rank_weights = ((3, 1.0), (4, 256.0), (5, 65536.0))
    column = dot(
        card,
        jnp.concatenate(
            [
                weigh(rank_weights, (META, 128), 0),
                weigh(((2, 1.0),), (META, 128), 0),
                weigh(((0, 1.0),), (META, 128), 0),
                weigh(((1, 1.0),), (META, 128), 0),
            ],
            axis=1,
        ),
    )
    rank, cluster = column[:, :128], column[:, 128:256]
    source, slot = column[:, 256:384], column[:, 384:]
    moved_rank = dot_nt(weigh(rank_weights, (8, META), 1), card)
    moved_cluster = dot_nt(weigh(((2, 1.0),), (8, META), 1), card)
    rank2 = jnp.concatenate([rank, rank], axis=1)
    cluster2 = jnp.concatenate([cluster, cluster], axis=1)

    unit = moved[:, :D]
    arrived = jnp.full((MOVED, 256), -1.0, F32)
    bests = []
    for j in range(ALL // 256):
        across = slice(j * 256, (j + 1) * 256)
        rows = got_ref[across, :D] if j * 256 < MAIN else late_ref[...]
        similar = dot_nt(unit, rows)
        same = cluster2 == row_ref[8:9, across]
        earlier = rank2 < row_ref[0:1, across]
        kept = jnp.where(same & earlier, similar, -1.0)
        here = jnp.maximum(best_ref[:, across], jnp.max(kept.reshape(32, 8, 256), axis=0))
        bests.append(jnp.max(here, axis=0, keepdims=True))
        later = rank2 > row_ref[0:1, across]
        arrived = jnp.maximum(arrived, jnp.where(same & later, similar, -1.0))
    similar = dot_nt(unit, unit)
    later = (cluster2 == moved_cluster[:1]) & (rank2 > moved_rank[:1])
    arrived = jnp.maximum(arrived, jnp.where(later, similar, -1.0))
    arrived = jnp.max(arrived, axis=1, keepdims=True)

    row_of = iota((N, MAIN), 0) == iota((N, MAIN), 1) // 8
    main = jnp.concatenate(bests[: MAIN // 256], axis=1)
    main = jnp.where(row_of, main, 0.0)
    out = dot(main, flag(iota((MAIN, N), 0) % 8 == iota((MAIN, N), 1), F32), HIGHEST)
    for k in range(2):
        late = bests[MAIN // 256][:, k * N : (k + 1) * N]
        late = jnp.where(iota((N, N), 0) == iota((N, N), 1), late, 0.0)
        out = out + dot(late, flag(iota((N, N), 1) == 8 + k, F32), HIGHEST)
    hop = jnp.where(iota((MOVED, N), 0) < NEAR, 1, 2)
    answers = jnp.where(
        (cluster > 0.0) & (iota((MOVED, N), 1) == hop * 16 + slot.astype(I32)), arrived, 0.0
    )
    sender = flag((cluster > 0.0) & (iota((MOVED, N), 1) == source.astype(I32)), F32)
    out = out + dot(sender.T, answers, HIGHEST)
    out_ref[...] = out


def cross_best(got, late, row, best, near, far):
    return pl.pallas_call(
        cross_kernel,
        out_shape=jax.ShapeDtypeStruct((N, N), F32),
        scratch_shapes=[pltpu.VMEM((MOVED, D + META), BF16)],
        compiler_params=LIMIT,
        name="cross_best",
    )(got, late, row, best, near, far)


def pick_kernel(back_ref, place_ref, out_ref):
    home = place_ref[0:1, :]
    lane = place_ref[1:2, :]
    table = dot(back_ref[...].T, flag(iota((N, ROWS), 0) == home, F32), HIGHEST)
    out_ref[...] = jnp.sum(
        jnp.where(iota((N, ROWS), 0) == lane, table, 0.0), axis=0, keepdims=True
    )


def pick(back, place):
    return pl.pallas_call(
        pick_kernel,
        out_shape=jax.ShapeDtypeStruct((1, ROWS), F32),
        compiler_params=LIMIT,
        name="pick",
    )(back, place)


def passed_along(array, by):
    return lax.ppermute(array, "dev", [(i, (i + by) % N) for i in range(N)])


def swapped(array):
    return lax.all_to_all(array, "dev", split_axis=0, concat_axis=0, tiled=True)


def paired_best(left, right):
    left_unit, left_cluster, left_rank = left
    right_unit, right_cluster, right_rank = right
    block_rows = 512
    block_count = left_unit.shape[0] // block_rows
    blocked = (
        left_unit.reshape(block_count, block_rows, D),
        left_cluster.reshape(block_count, block_rows),
        left_rank.reshape(block_count, block_rows),
    )

    def advance(carry, pieces):
        unit, cluster, rank = pieces
        similar = dot_nt(unit, right_unit)
        same = (cluster[:, None] == right_cluster[None, :]) & (right_cluster[None, :] >= 0)
        earlier = same & (right_rank[None, :] < rank[:, None])
        return carry, jnp.max(jnp.where(earlier, similar, -1.0), axis=1)

    return lax.scan(advance, 0, blocked)[1].reshape(-1)


def by_pools(emb, cluster, rank):
    capacity = 2 * ROWS // N
    pool_rows = N * capacity
    wide = emb.astype(F32)
    unit = (wide * lax.rsqrt(jnp.sum(wide * wide, axis=-1, keepdims=True) + 1e-06)).astype(BF16)
    target = (cluster % N + rank % 2) % N
    one_hot = (target[:, None] == jnp.arange(N, dtype=I32)[None, :]).astype(I32)
    slot = jnp.sum(jnp.cumsum(one_hot, axis=0) * one_hot, axis=1) - 1
    placing = target * capacity + slot
    received = (
        swapped(jnp.zeros((pool_rows, D), BF16).at[placing].set(unit)),
        swapped(jnp.full((pool_rows,), -1, I32).at[placing].set(cluster)),
        swapped(jnp.zeros((pool_rows,), I32).at[placing].set(rank)),
    )
    best = paired_best(received, received)
    for by in (1, -1):
        other = tuple(passed_along(part, by) for part in received)
        best = jnp.maximum(best, paired_best(received, other))
    return swapped(best)[placing]


def per_device(emb, cluster, rank):
    packed, place = pack(emb, cluster, rank)
    got = swapped(packed.reshape(N, 8, D + 256)).reshape(MAIN, D + 256)
    late, column, row, near, far, bad = unpack(got)
    near = passed_along(near, -1)
    far = passed_along(far, -2)
    best = local_best(got, late, column, row)
    answers = cross_best(got, late, row, best, near, far)
    back = swapped(answers.reshape(N, 1, N)).reshape(N, N)
    nearest = pick(back, place).reshape(ROWS)
    return lax.cond(
        bad[0, 0] > 0,
        by_pools,
        lambda emb, cluster, rank: nearest,
        emb,
        cluster,
        rank,
    )


def solution(mesh):
    placed = (P("dev", None), P("dev"), P("dev"))
    return jax.shard_map(
        per_device, mesh=mesh, in_specs=placed, out_specs=P("dev"), check_vma=False
    )
```

time: 204 us -> 87.8 us (0.43)
  matrix products: 51.2 us -> 0 us
  waiting for transfers between devices: 54.9 us -> 8.96 us
  starting transfers between devices: 35 us -> 10.3 us
  Pallas kernels: 0 us -> 22.8 us
  local copies, waits for them, and re-layouts: 24.6 us -> 2.54 us
  blocking collectives: 22.9 us -> 42.1 us
  other arithmetic: 14.7 us -> 0 us
    dot_general x12 -> x0, matrix products: 51.2 us -> none  [advance(): lax.dot_general(piece_unit, right_unit, (((1,), (1,)), ((), ())), preferr...]
    all_to_all x3 -> x1, waiting for transfers between devices: 35.5 us -> 8.96 us  [swapped(): return lax.all_to_all(array, 'dev', split_axis=0, concat_axis=0, tiled=True)]
    pallas_call x0 -> x5, Pallas kernels: none -> 22.8 us  [the longest x1 6.69 us: pack(): pl.pallas_call(pack_kernel, out_shape=(jax.ShapeDtypeStruct((MAIN, D + 25...]
    ppermute x6 -> x2, waiting for transfers between devices: 19.4 us -> 0.01 us  [passed_along(): return lax.ppermute(array, 'dev', [(i, (i + by) % N) for i in range(N)])]
    all_to_all x1, blocking collectives: 22.9 us -> 42.1 us  [swapped(): return lax.all_to_all(array, 'dev', split_axis=0, concat_axis=0, tiled=True)]
    all_to_all x3 -> x1, starting transfers between devices: 25.6 us -> 8.29 us  [swapped(): return lax.all_to_all(array, 'dev', split_axis=0, concat_axis=0, tiled=True)]
    gather x1 -> x0, local copies, waits for them, and re-layouts: 10.5 us -> none  [per_device(): return back_home[placing]]
    scatter x2 -> x0, local copies, waits for them, and re-layouts: 8.95 us -> none  [the longest x1 4.48 us: per_device(): jnp.full((pool_rows,), -1, jnp.int32).at[placing].set(cluster)]
  transfers between devices with their start and end apart: 9 -> 3, of which waited for: 5 -> 1; matrix products, arithmetic and copies ran while one was open for 26% -> 0% of each run, Pallas kernels for 0% -> 6%
where the time goes in v1:
time: 87.8 us; the launch traced here: 87.5 us
  blocking collectives  42.1 us (48%)
  Pallas kernels  22.8 us (26%)
  starting transfers between devices  10.3 us (12%)
  waiting for transfers between devices  8.96 us (10%)
  local copies, waits for them, and re-layouts  2.54 us (3%)
    all_to_all x1, blocking collectives, swapped(): return lax.all_to_all(array, 'dev', split_axis=0, concat_axis=0, tiled=True)  42.1 us
    all_to_all x1, waiting for transfers between devices, swapped(): return lax.all_to_all(array, 'dev', split_axis=0, concat_axis=0, tiled=True)  8.96 us
    all_to_all x1, starting transfers between devices, swapped(): return lax.all_to_all(array, 'dev', split_axis=0, concat_axis=0, tiled=True)  8.29 us
    pallas_call x1, Pallas kernels, pack(): pl.pallas_call(pack_kernel, out_shape=(jax.ShapeDtypeStruct((MAIN, D + 25...  6.69 us
    pallas_call x1, Pallas kernels, local_best(): pl.pallas_call(local_kernel, out_shape=jax.ShapeDtypeStruct((8, ALL), F32...  5.48 us
    pallas_call x1, Pallas kernels, unpack(): pl.pallas_call(unpack_kernel, out_shape=(jax.ShapeDtypeStruct((EXTRA, D),...  4.75 us
    pallas_call x1, Pallas kernels, cross_best(): pl.pallas_call(cross_kernel, out_shape=jax.ShapeDtypeStruct((N, N), F32),...  4.4 us
    unnamed x14, local copies, waits for them, and re-layouts  2.54 us
  transfers between devices with their start and end apart: 3, of which 1 were waited for; matrix products, arithmetic and copies ran while one was open for 0% of the time, Pallas kernels for 6%

profile of v1, /device:TPU:1, one launch (start us, length us, event | category | flops | bytes accessed | tf_op | source)
XLA Modules:
  0.0 87.5 jit_solution(2651927260676429110)
XLA Ops:
  0.0 6.7 %pack.1 = (bf16[1024,1024]{1,0:T(8,128)(2,1)}, s32[2,1024]{1,0:T(2,128)}) custom-call(bf16[1024,768]{1,0:T(8,128)(2,1)} %emb_ref.1, s32[1,1024]{1,0:T(1,128)} %bitcast.101, s32[1,1024]{1,0:T(1,128)} %bitcast.102), custom_call_target="tpu_custom_call" | custom-call | tf_op jit(solution)/shard_map/pack/pallas_call | solution.py:121
  6.7 42.1 %all_to_all.45 = bf16[128,8,1024]{2,1,0:T(8,128)(2,1)} all-to-all(bf16[128,8,1024]{2,1,0:T(8,128)(2,1)} %bitcast.85), channel_id=1, replica_groups=mesh['dev'=128] {'dev'}, dimensions={0} | all-to-all | bytes 4194304 | tf_op jit(solution)/shard_map/all_to_all | solution.py:383
  48.8 4.8 %unpack.1 = (bf16[256,768]{1,0:T(8,128)(2,1)}, f32[1280,256]{1,0:T(8,128)}, f32[16,1280]{1,0:T(8,128)}, bf16[176,896]{1,0:T(8,128)(2,1)}, bf16[16,896]{1,0:T(8,128)(2,1)}, /*index=5*/s32[1,1]{1,0:T(1,128)}) custom-call(bf16[1024,1024]{1,0:T(8,128)(2,1)} %bitcast.81), custom_call_target="tpu_custom_call" | custom-call | tf_op jit(solution)/shard_map/unpack/pallas_call | solution.py:227
  53.6 1.0 %collective-permute-start.6 = (bf16[176,896]{1,0:T(8,128)(2,1)}, bf16[176,896]{1,0:T(8,128)(2,1)S(1)}, u32[]{:S(2)}, u32[]{:S(2)}) collective-permute-start(bf16[176,896]{1,0:T(8,128)(2,1)} %get-tuple-element.159), channel_id=1, source_target_pairs={{0,127},{1,0},{2,1},{3,2},{4,3},{5,4},{6,5},{7,6},{8,7},{9,8},{10,... | collective-permute-start | bytes 946184 | tf_op jit(solution)/shard_map/ppermute | solution.py:379
  54.6 1.0 %collective-permute-start.7 = (bf16[16,896]{1,0:T(8,128)(2,1)}, bf16[16,896]{1,0:T(8,128)(2,1)S(1)}, u32[]{:S(2)}, u32[]{:S(2)}) collective-permute-start(bf16[16,896]{1,0:T(8,128)(2,1)} %get-tuple-element.160), channel_id=1, source_target_pairs={{0,126},{1,127},{2,0},{3,1},{4,2},{5,3},{6,4},{7,5},{8,6},{9,7},{1... | collective-permute-start | bytes 86024 | tf_op jit(solution)/shard_map/ppermute | solution.py:379
  55.5 5.5 %local_best.1.best_ref = f32[8,1280]{1,0:T(8,128)} custom-call(bf16[1024,1024]{1,0:T(8,128)(2,1)} %bitcast.82, bf16[256,768]{1,0:T(8,128)(2,1)} %get-tuple-element.156.late_ref, f32[1280,256]{1,0:T(8,128)} %get-tuple-element.158.column_ref, f32[16,1280]{1,0:T(8,128)} %get-tuple-element.157.row_ref), custom_call_target="tpu_custom_call" | custom-call | flops 2516582400 | bytes 3932160 | tf_op jit(solution)/shard_map/local_best/pallas_call | solution.py:270
  61.0 0.0 copy-start
  61.0 0.0 copy-start.4
  61.0 0.0 copy-start.5
  61.0 0.0 collective-permute-done.7.far_ref
  61.0 0.0 copy-start.3
  61.0 0.0 collective-permute-done.6.near_ref
  61.1 0.6 copy-done.3
  61.6 0.0 copy-start.1
  61.6 0.7 copy-done.1
  62.4 4.4 %cross_best.1 = f32[128,128]{1,0:T(8,128)} custom-call(bf16[1024,1024]{1,0:T(8,128)(2,1)} %bitcast.83, bf16[256,768]{1,0:T(8,128)(2,1)} %get-tuple-element.156.late_ref, f32[16,1280]{1,0:T(8,128)} %get-tuple-element.157.row_ref, f32[8,1280]{1,0:T(8,128)} %local_best.1.best_ref, bf16[176,896]{1,0:T(8,128)(2,1)} %copy-done.1, bf16[16,896]{1,0:T(8,128)(2,1)} %copy-done.3), custom_call_target="tpu_custom_call" | custom-call | tf_op jit(solution)/shard_map/cross_best/pallas_call | solution.py:351
  66.8 8.3 %all-to-all-start.5 = ((f32[128,1,128]{2,1,0:T(1,128)}), f32[128,1,128]{2,1,0:T(1,128)S(1)}, u32[]{:S(2)}, u32[]{:S(2)}) async-start(f32[128,1,128]{2,1,0:T(1,128)} %bitcast.88), calls=%async_computation.5 | async-start | bytes 131072 | tf_op jit(solution)/shard_map/all_to_all | solution.py:383
  75.7 9.0 %all-to-all-done.5 = f32[128,1,128]{2,1,0:T(1,128)S(1)} async-done(((f32[128,1,128]{2,1,0:T(1,128)}), f32[128,1,128]{2,1,0:T(1,128)S(1)}, u32[]{:S(2)}, u32[]{:S(2)}) %all-to-all-start.5) | async-done | bytes 65568 | tf_op jit(solution)/shard_map/all_to_all | solution.py:383
  84.7 0.0 copy-start.2
  84.7 0.6 copy-done.2
  85.3 1.5 %pick.1 = f32[1,1024]{1,0:T(1,128)S(1)} custom-call(f32[128,128]{1,0:T(8,128)} %bitcast.89, s32[2,1024]{1,0:T(2,128)} %get-tuple-element.161.place_ref), custom_call_target="tpu_custom_call" | custom-call | tf_op jit(solution)/shard_map/pick/pallas_call | solution.py:370
  86.8 0.0 copy-done
  86.8 0.0 copy-done.4
  86.8 0.0 copy-done.5
  86.9 0.0 copy-start.6
  86.9 0.6 copy-done.6
  (1 shorter events, 0.0 us)
Async XLA Ops:
  53.6 7.5 %collective-permute-start.6 = (bf16[176,896]{1,0:T(8,128)(2,1)}, bf16[176,896]{1,0:T(8,128)(2,1)S(1)}, u32[]{:S(2)}, u32[]{:S(2)}) collective-permute-start(bf16[176,896]{1,0:T(8,128)(2,1)} %get-tuple-element.159), channel_id=1, source_target_pairs={{0,127},{1,0},{2,1},{3,2},{4,3},{5,4},{6,5},{7,6},{8,7},{9,8},{10,... | collective-permute-start | bytes 946184 | tf_op jit(solution)/shard_map/ppermute | solution.py:379
  54.6 6.5 %collective-permute-start.7 = (bf16[16,896]{1,0:T(8,128)(2,1)}, bf16[16,896]{1,0:T(8,128)(2,1)S(1)}, u32[]{:S(2)}, u32[]{:S(2)}) collective-permute-start(bf16[16,896]{1,0:T(8,128)(2,1)} %get-tuple-element.160), channel_id=1, source_target_pairs={{0,126},{1,127},{2,0},{3,1},{4,2},{5,3},{6,4},{7,5},{8,6},{9,7},{1... | collective-permute-start | bytes 86024 | tf_op jit(solution)/shard_map/ppermute | solution.py:379
  61.0 25.8 %copy-start = (bf16[1024,768]{1,0:T(8,128)(2,1)S(1)}, bf16[1024,768]{1,0:T(8,128)(2,1)}, u32[]{:S(2)}) copy-start(bf16[1024,768]{1,0:T(8,128)(2,1)} %emb_ref.1) | copy-start | bytes 4718596
  61.0 25.8 %copy-start.4 = (s32[1024]{0:T(1024)S(1)}, s32[1024]{0:T(1024)}, u32[]{:S(2)}) copy-start(s32[1024]{0:T(1024)} %param.12) | copy-start | bytes 12292
  61.0 25.8 %copy-start.5 = (s32[1024]{0:T(1024)S(1)}, s32[1024]{0:T(1024)}, u32[]{:S(2)}) copy-start(s32[1024]{0:T(1024)} %param.13) | copy-start | bytes 12292
  61.0 0.6 copy-start.3
  61.6 0.7 copy-start.1
  66.8 17.9 %all-to-all-start.5 = ((f32[128,1,128]{2,1,0:T(1,128)}), f32[128,1,128]{2,1,0:T(1,128)S(1)}, u32[]{:S(2)}, u32[]{:S(2)}) async-start(f32[128,1,128]{2,1,0:T(1,128)} %bitcast.88), calls=%async_computation.5 | async-start | bytes 131072 | tf_op jit(solution)/shard_map/all_to_all | solution.py:383
  84.7 0.6 copy-start.2
  86.9 0.6 copy-start.6

commit v2 on v1

v2 whole, which is shorter than its diff:
```python
import functools

import jax
import jax.numpy as jnp
from jax import lax
from jax.experimental import pallas as pl
from jax.experimental.pallas import tpu as pltpu
from jax.sharding import PartitionSpec as P

F32 = jnp.float32
BF16 = jnp.bfloat16
I32 = jnp.int32

N = 128
ROWS = 1024
D = 768
SLOTS = 10
MAIN = 8 * N
EXTRA = 2 * N
ALL = MAIN + EXTRA
NEAR = 144
FAR = 16
MOVED = NEAR + FAR
META = 128
LIMIT = pltpu.CompilerParams(vmem_limit_bytes=20 * 1024 * 1024)


def iota(shape, dim):
    return lax.broadcasted_iota(I32, shape, dim)


def flag(mask, dtype=BF16):
    return jnp.where(mask, 1.0, 0.0).astype(dtype)


def dot(a, b):
    return jnp.dot(a, b, preferred_element_type=F32)


def dot_nt(a, b):
    return lax.dot_general(a, b, (((1,), (1,)), ((), ())), preferred_element_type=F32)


def parts(a):
    high = a.astype(BF16)
    rest = a - high.astype(F32)
    middle = rest.astype(BF16)
    return high, middle, (rest - middle.astype(F32)).astype(BF16)


def weights(rows, shape, dim, size=16):
    group = iota(shape, dim) // size
    weight = jnp.zeros(shape, F32)
    for at, by in rows:
        weight = jnp.where(group == at, by, weight)
    return weight.astype(BF16)


def pack_kernel(
    emb_ref, cluster_ref, rank_ref, out_ref, place_ref, raw, unit, left, right, arrived
):
    loads = [
        pltpu.make_async_copy(
            emb_ref.at[pl.ds(c * 256, 256), :], raw.at[pl.ds(c * 256, 256), :], arrived.at[c]
        )
        for c in range(4)
    ]
    for load in loads:
        load.start()

    cluster = cluster_ref[...]
    rank = rank_ref[...]
    home = cluster & (N - 1)
    member = cluster // N

    which = iota((N, ROWS), 0)
    at_home = which == home
    at_home_b = flag(at_home)
    count = dot_nt(jnp.ones((8, ROWS), BF16), at_home_b)
    chunks = jnp.concatenate([at_home_b[:, c * 128 : (c + 1) * 128] for c in range(8)], axis=0)
    lower = flag(iota((128, 128), 0) <= iota((128, 128), 1))
    running = dot(chunks, jnp.concatenate([lower, jnp.ones((128, 128), BF16)], axis=1))

    window = count - float(SLOTS)
    queue = jnp.maximum(window, 0.0)
    for step in (1, 2, 4, 8, 16, 32, 64):
        queue = jnp.maximum(queue, window + pltpu.roll(queue, step, 1))
        window = window + pltpu.roll(window, step, 1)
    ahead = pltpu.roll(queue, 1, 1)
    ahead_high = jnp.floor(ahead * (1.0 / 256.0)) * 256.0
    ahead = dot(jnp.concatenate([ahead_high, ahead - ahead_high], axis=0).astype(BF16), at_home_b)
    ahead = ahead[0:1] + ahead[8:9]

    before = jnp.zeros((128, 128), F32)
    turn = []
    for c in range(8):
        part = running[c * 128 : (c + 1) * 128]
        turn.append(
            jnp.sum(
                jnp.where(at_home[:, c * 128 : (c + 1) * 128], part[:, :128] + before, 0.0),
                axis=0,
                keepdims=True,
            )
        )
        before = before + part[:, 128:]
    offset = jnp.concatenate(turn, axis=1) - 1.0 + ahead
    hops = jnp.floor((offset + 0.5) * (1.0 / SLOTS))
    slot = (offset - hops * SLOTS).astype(I32)
    hops = hops.astype(I32)
    target = (home + hops) & (N - 1)
    place_ref[0:1, :] = home
    place_ref[1:2, :] = jnp.minimum(hops, 7) * 16 + slot

    for c in range(4):
        loads[c].wait()
        wide = raw[c * 256 : (c + 1) * 256, :].astype(F32)
        scale = lax.rsqrt(jnp.sum(wide * wide, axis=-1, keepdims=True) + 1e-06)
        unit[c * 256 : (c + 1) * 256, :] = (wide * scale).astype(BF16)

    def spread(value):
        return jnp.broadcast_to(value, (16, ROWS))

    value = jnp.concatenate(
        [
            spread(member + 1),
            spread(hops),
            spread(rank & 255),
            spread((rank >> 8) & 255),
            spread(rank >> 16),
            jnp.zeros((48, ROWS), I32),
        ],
        axis=0,
    )
    value = jnp.where((iota((META, ROWS), 0) & 15) == slot, value, 0)
    meta = dot_nt(flag(which == target), value.astype(F32).astype(BF16))
    left[pl.ds(6, N, stride=8), :] = meta
    right[pl.ds(6, N, stride=8), :] = jnp.broadcast_to(jnp.minimum(queue[:1], 255.0), (N, 128))
    left[pl.ds(7, N, stride=8), :] = jnp.zeros((N, 128), F32)
    right[pl.ds(7, N, stride=8), :] = jnp.zeros((N, 128), F32)
    extra_row = jnp.where(slot >= 8, (slot - 8) * N + target, -1)
    late = dot(flag(iota((EXTRA, ROWS), 0) == extra_row), unit[...])
    for k in range(2):
        for piece in range(3):
            rows = late[k * N : (k + 1) * N, piece * 256 : (piece + 1) * 256]
            left[pl.ds(2 * piece + k, N, stride=8), :] = rows[:, :128]
            right[pl.ds(2 * piece + k, N, stride=8), :] = rows[:, 128:]
    out_ref[:, D : D + 128] = left[...].astype(BF16)
    out_ref[:, D + 128 :] = right[...].astype(BF16)

    main_row = jnp.where(slot < 8, target * 8 + slot, -1)
    for b in range(4):
        chosen = flag(iota((256, ROWS), 0) == main_row - b * 256)
        out_ref[b * 256 : (b + 1) * 256, :D] = dot(chosen, unit[...]).astype(BF16)


def pack(emb, cluster, rank):
    return pl.pallas_call(
        pack_kernel,
        in_specs=[
            pl.BlockSpec(memory_space=pl.ANY),
            pl.BlockSpec(memory_space=pltpu.VMEM),
            pl.BlockSpec(memory_space=pltpu.VMEM),
        ],
        out_shape=(
            jax.ShapeDtypeStruct((MAIN, D + 256), BF16),
            jax.ShapeDtypeStruct((2, ROWS), I32),
        ),
        scratch_shapes=[
            pltpu.VMEM((ROWS, D), BF16),
            pltpu.VMEM((ROWS, D), BF16),
            pltpu.VMEM((MAIN, 128), F32),
            pltpu.VMEM((MAIN, 128), F32),
            pltpu.SemaphoreType.DMA((4,)),
        ],
        compiler_params=LIMIT,
        name="pack",
    )(emb, cluster.reshape(1, ROWS), rank.reshape(1, ROWS))


def unpack_kernel(got_ref, late_ref, meta_ref, near_ref, far_ref, bad_ref, left, right):
    left[...] = got_ref[:, D : D + 128].astype(F32)
    right[...] = got_ref[:, D + 128 :].astype(F32)
    for k in range(2):
        for piece in range(3):
            for half, ref in enumerate((left, right)):
                at = piece * 256 + half * 128
                late_ref[k * N : (k + 1) * N, at : at + 128] = ref[
                    pl.ds(2 * piece + k, N, stride=8), :
                ].astype(BF16)
    meta = left[pl.ds(6, N, stride=8), :]
    queue = right[pl.ds(6, N, stride=8), :]
    meta_ref[...] = meta

    over_near = jnp.sum(jnp.minimum(queue, float(SLOTS)), axis=0, keepdims=True) - NEAR
    over_far = (
        jnp.sum(jnp.clip(queue - SLOTS, 0.0, float(SLOTS)), axis=0, keepdims=True) - FAR
    )
    over_long = jnp.max(queue, axis=0, keepdims=True) - 2.0 * SLOTS
    bad_ref[0, 0] = (
        jnp.max(jnp.maximum(jnp.maximum(over_near, over_far), over_long)) > 0.0
    ).astype(I32)

    lane = iota((N, N), 1)
    hops = pltpu.roll(meta, N - 16, 1)
    moves = (lane < SLOTS) & (meta > 0.0)
    one = flag(moves & (hops == 1.0))
    two = flag(moves & (hops == 2.0))
    each = dot_nt(jnp.ones((8, N), BF16), jnp.concatenate([one, two], axis=0))
    first = dot(
        jnp.concatenate([each[:, :N], each[:, N:]], axis=0).astype(BF16),
        flag(iota((N, N), 0) < iota((N, N), 1)),
    )
    count_one, count_two = each[0:1, :N], each[0:1, N:]
    first_one, first_two = first[0:1], first[8:9]

    def rows_of(length, first, count, skip):
        line = iota((length, N), 0).astype(F32)
        mine = (line >= first) & (line < first + count)
        source = jnp.sum(jnp.where(mine, iota((length, N), 1).astype(F32), 0.0), 1, keepdims=True)
        place = jnp.sum(jnp.where(mine, line - first + skip, 0.0), 1, keepdims=True)
        any_row = line[:, :1] < jnp.sum(count, 1, keepdims=True)
        return flag(mine), source.astype(I32), place.astype(I32), any_row

    near = rows_of(NEAR, first_one, count_one, count_two)
    far = rows_of(FAR, first_two, count_two, 0.0)
    mine, source, slot = (jnp.concatenate([a, b], axis=0) for a, b in zip(near[:3], far[:3]))
    used = jnp.concatenate([near[3].astype(I32), far[3].astype(I32)], axis=0) > 0

    at_main = jnp.where(used & (slot < 8), source * 8 + slot, -1)
    at_late = jnp.where(used & (slot >= 8), (slot - 8) * N + source, -1)
    sent = dot(flag(iota((MOVED, MAIN), 1) == at_main), got_ref[:, :D]) + dot(
        flag(iota((MOVED, EXTRA), 1) == at_late), late_ref[...]
    )
    sent = sent.astype(BF16)
    card = dot(mine, meta.astype(BF16))
    lanes = iota((MOVED, META), 1)
    card = jnp.where((lanes & 15) == slot, card, 0.0)
    card = jnp.where(lanes == 96, source.astype(F32), card)
    card = jnp.where(lanes == 97, slot.astype(F32), card).astype(BF16)
    near_ref[:, :D] = sent[:NEAR]
    near_ref[:, D:] = card[:NEAR]
    far_ref[:, :D] = sent[NEAR:]
    far_ref[:, D:] = card[NEAR:]


def unpack(got):
    return pl.pallas_call(
        unpack_kernel,
        out_shape=(
            jax.ShapeDtypeStruct((EXTRA, D), BF16),
            jax.ShapeDtypeStruct((N, META), F32),
            jax.ShapeDtypeStruct((NEAR, D + META), BF16),
            jax.ShapeDtypeStruct((FAR, D + META), BF16),
            jax.ShapeDtypeStruct((1, 1), I32),
        ),
        out_specs=(pl.BlockSpec(memory_space=pltpu.VMEM),) * 4
        + (pl.BlockSpec(memory_space=pltpu.SMEM),),
        scratch_shapes=[pltpu.VMEM((MAIN, 128), F32), pltpu.VMEM((MAIN, 128), F32)],
        compiler_params=LIMIT,
        name="unpack",
    )(got)


RANK = ((2, 1.0), (3, 256.0), (4, 65536.0))
CLUSTER = ((0, 1.0), (1, -16.0))


def local_kernel(got_ref, late_ref, meta_ref, row_ref, best_ref, own, column):
    meta = meta_ref[...]
    spread = dot(flag((iota((MAIN, N), 0) >> 3) == iota((MAIN, N), 1)), meta.astype(BF16))
    own[:MAIN, :] = jnp.where(
        (iota((MAIN, N), 1) & 15) == (iota((MAIN, N), 0) & 7), spread, 0.0
    ).astype(BF16)
    lane = iota((N, N), 1) & 15
    for k in range(2):
        own[MAIN + k * N : MAIN + (k + 1) * N, :] = jnp.where(lane == 8 + k, meta, 0.0).astype(BF16)
    row_ref[...] = dot_nt(
        jnp.concatenate([weights(RANK, (8, N), 1), weights(CLUSTER, (8, N), 1)], axis=0), own[...]
    )
    column[...] = dot(
        own[...],
        jnp.concatenate([weights(RANK, (N, N), 0), weights(CLUSTER, (N, N), 0)], axis=1),
    )
    best_ref[...] = jnp.full((8, ALL), -1.0, F32)

    def rows_of(b):
        if b * 256 < MAIN:
            return got_ref[b * 256 : (b + 1) * 256, :D]
        return late_ref[...]

    blocks = ALL // 256
    for i in range(blocks):
        rank = column[i * 256 : (i + 1) * 256, :128]
        cluster = column[i * 256 : (i + 1) * 256, 128:]
        rank = jnp.concatenate([rank, rank], axis=1)
        cluster = jnp.concatenate([cluster, cluster], axis=1)
        for j in range(blocks):
            across = slice(j * 256, (j + 1) * 256)
            similar = dot_nt(rows_of(i), rows_of(j))
            earlier = (cluster == row_ref[8:9, across]) & (rank < row_ref[0:1, across])
            kept = jnp.where(earlier, similar, -1.0)
            best_ref[:, across] = jnp.maximum(
                best_ref[:, across], jnp.max(kept.reshape(32, 8, 256), axis=0)
            )


def local_best(got, late, meta):
    return pl.pallas_call(
        local_kernel,
        out_shape=(
            jax.ShapeDtypeStruct((16, ALL), F32),
            jax.ShapeDtypeStruct((8, ALL), F32),
        ),
        scratch_shapes=[pltpu.VMEM((ALL, N), BF16), pltpu.VMEM((ALL, 256), F32)],
        compiler_params=LIMIT,
        cost_estimate=pl.CostEstimate(
            flops=2 * ALL * ALL * D, bytes_accessed=4 * ALL * D, transcendentals=0
        ),
        name="local_best",
    )(got, late, meta)


def cross_kernel(got_ref, late_ref, row_ref, best_ref, near_ref, far_ref, out_ref, moved):
    moved[0:NEAR, :] = near_ref[...]
    moved[NEAR:, :] = far_ref[...]
    card = moved[:, D:]
    column = dot(
        card,
        jnp.concatenate(
            [
                weights(RANK, (META, 128), 0),
                weights(CLUSTER[:1], (META, 128), 0),
                weights(((96, 1.0),), (META, 128), 0, 1),
                weights(((97, 1.0),), (META, 128), 0, 1),
            ],
            axis=1,
        ),
    )
    rank, cluster = column[:, :128], column[:, 128:256]
    source, slot = column[:, 256:384].astype(I32), column[:, 384:].astype(I32)
    moved_row = dot_nt(
        jnp.concatenate([weights(RANK, (8, META), 1), weights(CLUSTER[:1], (8, META), 1)], axis=0),
        card,
    )
    rank2 = jnp.concatenate([rank, rank], axis=1)
    cluster2 = jnp.concatenate([cluster, cluster], axis=1)

    unit = moved[:, :D]
    arrived = jnp.full((MOVED, 256), -1.0, F32)
    bests = []
    for j in range(ALL // 256):
        across = slice(j * 256, (j + 1) * 256)
        rows = got_ref[across, :D] if j * 256 < MAIN else late_ref[...]
        similar = dot_nt(unit, rows)
        same = cluster2 == row_ref[8:9, across]
        earlier = rank2 < row_ref[0:1, across]
        kept = jnp.where(same & earlier, similar, -1.0)
        here = jnp.maximum(best_ref[:, across], jnp.max(kept.reshape(MOVED // 8, 8, 256), axis=0))
        bests.append(jnp.max(here, axis=0, keepdims=True))
        later = rank2 > row_ref[0:1, across]
        arrived = jnp.maximum(arrived, jnp.where(same & later, similar, -1.0))
    similar = dot_nt(unit, unit)
    later = (cluster2[:, :MOVED] == moved_row[8:9]) & (rank2[:, :MOVED] > moved_row[0:1])
    arrived = jnp.maximum(
        jnp.max(arrived, axis=1, keepdims=True),
        jnp.max(jnp.where(later, similar, -1.0), axis=1, keepdims=True),
    )

    main = jnp.concatenate(bests[: MAIN // 256], axis=1)
    main = jnp.where((iota((8, MAIN), 1) & 7) == iota((8, MAIN), 0), main, 0.0)
    of_sender = flag((iota((MAIN, N), 0) >> 3) == iota((MAIN, N), 1))
    answers = sum(dot(part, of_sender) for part in parts(main))
    late = bests[MAIN // 256]
    answers = jnp.concatenate(
        [answers, late[:, :N], late[:, N:], jnp.zeros((N - SLOTS, N), F32)], axis=0
    )
    hop = jnp.where(iota((MOVED, N), 0) < NEAR, 16, 32)
    by_lane = jnp.where((cluster > 0.0) & (iota((MOVED, N), 1) == hop + slot), arrived, 0.0)
    sender = flag((cluster > 0.0) & (iota((MOVED, N), 1) == source), F32).T.astype(BF16)
    out_ref[...] = answers.T + sum(dot(sender, part) for part in parts(by_lane))


def cross_best(got, late, row, best, near, far):
    return pl.pallas_call(
        cross_kernel,
        out_shape=jax.ShapeDtypeStruct((N, N), F32),
        scratch_shapes=[pltpu.VMEM((MOVED, D + META), BF16)],
        compiler_params=LIMIT,
        name="cross_best",
    )(got, late, row, best, near, far)


def pick_kernel(back_ref, place_ref, out_ref):
    home = place_ref[0:1, :]
    lane = place_ref[1:2, :]
    at_home = flag(iota((N, ROWS), 0) == home)
    table = sum(dot(part, at_home) for part in parts(back_ref[...].T[:48]))
    out_ref[...] = jnp.sum(
        jnp.where(iota((48, ROWS), 0) == lane, table, 0.0), axis=0, keepdims=True
    )


def pick(back, place):
    return pl.pallas_call(
        pick_kernel,
        out_shape=jax.ShapeDtypeStruct((1, ROWS), F32),
        compiler_params=LIMIT,
        name="pick",
    )(back, place)


def passed_along(array, by):
    return lax.ppermute(array, "dev", [(i, (i + by) % N) for i in range(N)])


def swapped(array):
    return lax.all_to_all(array, "dev", split_axis=0, concat_axis=0, tiled=True)


def paired_best(left, right):
    left_unit, left_cluster, left_rank = left
    right_unit, right_cluster, right_rank = right
    block_rows = 512
    block_count = left_unit.shape[0] // block_rows
    blocked = (
        left_unit.reshape(block_count, block_rows, D),
        left_cluster.reshape(block_count, block_rows),
        left_rank.reshape(block_count, block_rows),
    )

    def advance(carry, pieces):
        unit, cluster, rank = pieces
        similar = dot_nt(unit, right_unit)
        same = (cluster[:, None] == right_cluster[None, :]) & (right_cluster[None, :] >= 0)
        earlier = same & (right_rank[None, :] < rank[:, None])
        return carry, jnp.max(jnp.where(earlier, similar, -1.0), axis=1)

    return lax.scan(advance, 0, blocked)[1].reshape(-1)


def by_pools(emb, cluster, rank):
    capacity = 2 * ROWS // N
    pool_rows = N * capacity
    wide = emb.astype(F32)
    unit = (wide * lax.rsqrt(jnp.sum(wide * wide, axis=-1, keepdims=True) + 1e-06)).astype(BF16)
    target = (cluster % N + rank % 2) % N
    one_hot = (target[:, None] == jnp.arange(N, dtype=I32)[None, :]).astype(I32)
    slot = jnp.sum(jnp.cumsum(one_hot, axis=0) * one_hot, axis=1) - 1
    placing = target * capacity + slot
    received = (
        swapped(jnp.zeros((pool_rows, D), BF16).at[placing].set(unit)),
        swapped(jnp.full((pool_rows,), -1, I32).at[placing].set(cluster)),
        swapped(jnp.zeros((pool_rows,), I32).at[placing].set(rank)),
    )
    best = paired_best(received, received)
    for by in (1, -1):
        other = tuple(passed_along(part, by) for part in received)
        best = jnp.maximum(best, paired_best(received, other))
    return swapped(best)[placing]


def per_device(emb, cluster, rank):
    packed, place = pack(emb, cluster, rank)
    got = swapped(packed.reshape(N, 8, D + 256)).reshape(MAIN, D + 256)
    late, meta, near, far, bad = unpack(got)
    near = passed_along(near, -1)
    far = passed_along(far, -2)
    row, best = local_best(got, late, meta)
    answers = cross_best(got, late, row, best, near, far)
    back = swapped(answers.reshape(N, 1, N)).reshape(N, N)
    nearest = pick(back, place).reshape(ROWS)
    return lax.cond(
        bad[0, 0] > 0,
        by_pools,
        lambda emb, cluster, rank: nearest,
        emb,
        cluster,
        rank,
    )


def solution(mesh):
    placed = (P("dev", None), P("dev"), P("dev"))
    return jax.shard_map(
        per_device, mesh=mesh, in_specs=placed, out_specs=P("dev"), check_vma=False
    )
```

time: 87.8 us -> 76 us (0.87)
  Pallas kernels: 22.8 us -> 12 us
  local copies, waits for them, and re-layouts: 2.54 us -> 0.61 us
    pallas_call x2, Pallas kernels: 12.2 us -> 8.26 us  [the longest x1 4.85 us: pack(): pl.pallas_call(pack_kernel, in_specs=[pl.BlockSpec(memory_space=pl.ANY),...]
    pallas_call x1, Pallas kernels: 4.75 us -> 1.56 us  [unpack(): pl.pallas_call(unpack_kernel, out_shape=(jax.ShapeDtypeStruct((EXTRA, D),...]
    pallas_call x1, Pallas kernels: 4.4 us -> 1.82 us  [cross_best(): pl.pallas_call(cross_kernel, out_shape=jax.ShapeDtypeStruct((N, N), F32),...]
    unnamed x14 -> x8, local copies, waits for them, and re-layouts: 2.54 us -> 0.61 us
    pallas_call x1, Pallas kernels: 1.49 us -> 0.32 us  [pick(): pl.pallas_call(pick_kernel, out_shape=jax.ShapeDtypeStruct((1, ROWS), F32...]
  transfers between devices with their start and end apart: 3 -> 3, of which waited for: 1 -> 2; matrix products, arithmetic and copies ran while one was open for 0% -> 0% of each run, Pallas kernels for 6% -> 5%
where the time goes in v2:
time: 76 us; the launch traced here: 75.8 us
  blocking collectives  41.8 us (55%)
  Pallas kernels  12 us (16%)
  starting transfers between devices  10.8 us (14%)
  waiting for transfers between devices  9.66 us (13%)
  between operations  0.76 us (1%)
    all_to_all x1, blocking collectives, swapped(): return lax.all_to_all(array, 'dev', split_axis=0, concat_axis=0, tiled=True)  41.8 us
    all_to_all x1, waiting for transfers between devices, swapped(): return lax.all_to_all(array, 'dev', split_axis=0, concat_axis=0, tiled=True)  8.96 us
    all_to_all x1, starting transfers between devices, swapped(): return lax.all_to_all(array, 'dev', split_axis=0, concat_axis=0, tiled=True)  8.79 us
    pallas_call x1, Pallas kernels, pack(): pl.pallas_call(pack_kernel, in_specs=[pl.BlockSpec(memory_space=pl.ANY),...  4.85 us
    pallas_call x1, Pallas kernels, local_best(): pl.pallas_call(local_kernel, out_shape=(jax.ShapeDtypeStruct((16, ALL), F...  3.42 us
    ppermute x2, starting transfers between devices, passed_along(): return lax.ppermute(array, 'dev', [(i, (i + by) % N) for i in range(N)])  1.96 us
    pallas_call x1, Pallas kernels, cross_best(): pl.pallas_call(cross_kernel, out_shape=jax.ShapeDtypeStruct((N, N), F32),...  1.82 us
    pallas_call x1, Pallas kernels, unpack(): pl.pallas_call(unpack_kernel, out_shape=(jax.ShapeDtypeStruct((EXTRA, D),...  1.56 us
  transfers between devices with their start and end apart: 3, of which 2 were waited for; matrix products, arithmetic and copies ran while one was open for 0% of the time, Pallas kernels for 5%

profile of v2, /device:TPU:1, one launch (start us, length us, event | category | flops | bytes accessed | tf_op | source)
XLA Modules:
  0.0 75.8 jit_solution(268526216255964147)
XLA Ops:
  0.0 4.8 %pack.1 = (bf16[1024,1024]{1,0:T(8,128)(2,1)S(1)}, s32[2,1024]{1,0:T(2,128)S(1)}) custom-call(bf16[1024,768]{1,0:T(8,128)(2,1)} %emb_ref.1, s32[1,1024]{1,0:T(1,128)} %bitcast.100, s32[1,1024]{1,0:T(1,128)} %bitcast.101), custom_call_target="tpu_custom_call" | custom-call | tf_op jit(solution)/shard_map/pack/pallas_call | solution.py:157
  4.9 41.8 %all_to_all.45 = bf16[128,8,1024]{2,1,0:T(8,128)(2,1)S(1)} all-to-all(bf16[128,8,1024]{2,1,0:T(8,128)(2,1)S(1)} %bitcast.84), channel_id=1, replica_groups=mesh['dev'=128] {'dev'}, dimensions={0} | all-to-all | bytes 4194304 | tf_op jit(solution)/shard_map/all_to_all | solution.py:417
  46.7 1.6 %unpack.1 = (bf16[256,768]{1,0:T(8,128)(2,1)S(1)}, f32[128,128]{1,0:T(8,128)S(1)}, bf16[144,896]{1,0:T(8,128)(2,1)S(1)}, bf16[16,896]{1,0:T(8,128)(2,1)S(1)}, s32[1,1]{1,0:T(1,128)}) custom-call(bf16[1024,1024]{1,0:T(8,128)(2,1)S(1)} %bitcast.81), custom_call_target="tpu_custom_call" | custom-call | tf_op jit(solution)/shard_map/unpack/pallas_call | solution.py:247
  48.2 1.0 %collective-permute-start.6 = (bf16[144,896]{1,0:T(8,128)(2,1)S(1)}, bf16[144,896]{1,0:T(8,128)(2,1)S(1)}, u32[]{:S(2)}, u32[]{:S(2)}) collective-permute-start(bf16[144,896]{1,0:T(8,128)(2,1)S(1)} %get-tuple-element.161), channel_id=1, source_target_pairs={{0,127},{1,0},{2,1},{3,2},{4,3},{5,4},{6,5},{7,6},{8,7},{9,8},{10,... | collective-permute-start | bytes 774152 | tf_op jit(solution)/shard_map/ppermute | solution.py:413
  49.2 1.0 %collective-permute-start.7 = (bf16[16,896]{1,0:T(8,128)(2,1)S(1)}, bf16[16,896]{1,0:T(8,128)(2,1)S(1)}, u32[]{:S(2)}, u32[]{:S(2)}) collective-permute-start(bf16[16,896]{1,0:T(8,128)(2,1)S(1)} %get-tuple-element.162), channel_id=1, source_target_pairs={{0,126},{1,127},{2,0},{3,1},{4,2},{5,3},{6,4},{7,5},{8,6},{9,7},{1... | collective-permute-start | bytes 86024 | tf_op jit(solution)/shard_map/ppermute | solution.py:413
  50.2 3.4 %local_best.1 = (f32[16,1280]{1,0:T(8,128)S(1)}, f32[8,1280]{1,0:T(8,128)S(1)}) custom-call(bf16[1024,1024]{1,0:T(8,128)(2,1)S(1)} %bitcast.82, bf16[256,768]{1,0:T(8,128)(2,1)S(1)} %get-tuple-element.157.late_ref, f32[128,128]{1,0:T(8,128)S(1)} %get-tuple-element.158.meta_ref), custom_call_target="tpu_custom_call" | custom-call | flops 2516582400 | bytes 3932160 | tf_op jit(solution)/shard_map/local_best/pallas_call | solution.py:308
  53.6 0.0 copy-start
  53.6 0.0 copy-start.1
  53.7 0.0 copy-start.2
  53.7 0.0 collective-permute-done.7.far_ref
  53.7 0.7 collective-permute-done.6.near_ref
  54.4 1.8 %cross_best.1 = f32[128,128]{1,0:T(8,128)} custom-call(bf16[1024,1024]{1,0:T(8,128)(2,1)S(1)} %bitcast.83, bf16[256,768]{1,0:T(8,128)(2,1)S(1)} %get-tuple-element.157.late_ref, f32[16,1280]{1,0:T(8,128)S(1)} %get-tuple-element.159.row_ref, f32[8,1280]{1,0:T(8,128)S(1)} %get-tuple-element.160.best_ref, bf16[144,896]{1,0:T(8,128)(2,1)S(1)} %collective-permute-done.6.near_ref, ...), custom_call_target="tpu_custom_call" | custom-call | tf_op jit(solution)/shard_map/cross_best/pallas_call | solution.py:384
  56.2 8.8 %all-to-all-start.5 = ((f32[128,1,128]{2,1,0:T(1,128)}), f32[128,1,128]{2,1,0:T(1,128)S(1)}, u32[]{:S(2)}, u32[]{:S(2)}) async-start(f32[128,1,128]{2,1,0:T(1,128)} %bitcast.29), calls=%async_computation.5 | async-start | bytes 131072 | tf_op jit(solution)/shard_map/all_to_all | solution.py:417
  65.6 9.0 %all-to-all-done.5 = f32[128,1,128]{2,1,0:T(1,128)S(1)} async-done(((f32[128,1,128]{2,1,0:T(1,128)}), f32[128,1,128]{2,1,0:T(1,128)S(1)}, u32[]{:S(2)}, u32[]{:S(2)}) %all-to-all-start.5) | async-done | bytes 65568 | tf_op jit(solution)/shard_map/all_to_all | solution.py:417
  74.6 0.3 pick.1
  74.9 0.0 copy-done
  74.9 0.0 copy-done.1
  74.9 0.0 copy-done.2
  74.9 0.2 conditional.1
  75.2 0.0 copy-start.3
  75.2 0.6 copy-done.3
Async XLA Ops:
  48.2 6.1 %collective-permute-start.6 = (bf16[144,896]{1,0:T(8,128)(2,1)S(1)}, bf16[144,896]{1,0:T(8,128)(2,1)S(1)}, u32[]{:S(2)}, u32[]{:S(2)}) collective-permute-start(bf16[144,896]{1,0:T(8,128)(2,1)S(1)} %get-tuple-element.161), channel_id=1, source_target_pairs={{0,127},{1,0},{2,1},{3,2},{4,3},{5,4},{6,5},{7,6},{8,7},{9,8},{10,... | collective-permute-start | bytes 774152 | tf_op jit(solution)/shard_map/ppermute | solution.py:413
  49.2 4.4 %collective-permute-start.7 = (bf16[16,896]{1,0:T(8,128)(2,1)S(1)}, bf16[16,896]{1,0:T(8,128)(2,1)S(1)}, u32[]{:S(2)}, u32[]{:S(2)}) collective-permute-start(bf16[16,896]{1,0:T(8,128)(2,1)S(1)} %get-tuple-element.162), channel_id=1, source_target_pairs={{0,126},{1,127},{2,0},{3,1},{4,2},{5,3},{6,4},{7,5},{8,6},{9,7},{1... | collective-permute-start | bytes 86024 | tf_op jit(solution)/shard_map/ppermute | solution.py:413
  53.6 21.3 %copy-start = (bf16[1024,768]{1,0:T(8,128)(2,1)S(1)}, bf16[1024,768]{1,0:T(8,128)(2,1)}, u32[]{:S(2)}) copy-start(bf16[1024,768]{1,0:T(8,128)(2,1)} %emb_ref.1) | copy-start | bytes 4718596
  53.6 21.3 %copy-start.1 = (s32[1024]{0:T(1024)S(1)}, s32[1024]{0:T(1024)}, u32[]{:S(2)}) copy-start(s32[1024]{0:T(1024)} %param.12) | copy-start | bytes 12292
  53.7 21.3 %copy-start.2 = (s32[1024]{0:T(1024)S(1)}, s32[1024]{0:T(1024)}, u32[]{:S(2)}) copy-start(s32[1024]{0:T(1024)} %param.13) | copy-start | bytes 12292
  56.2 18.4 %all-to-all-start.5 = ((f32[128,1,128]{2,1,0:T(1,128)}), f32[128,1,128]{2,1,0:T(1,128)S(1)}, u32[]{:S(2)}, u32[]{:S(2)}) async-start(f32[128,1,128]{2,1,0:T(1,128)} %bitcast.29), calls=%async_computation.5 | async-start | bytes 131072 | tf_op jit(solution)/shard_map/all_to_all | solution.py:417
  75.2 0.6 copy-start.3

commit v3 on v2

--- a/solution.py
+++ b/solution.py
@@ -56,6 +56,18 @@
     return weight.astype(BF16)
 
 
+RING_Y = 1878693120
+RING_Z = 29252580
+
+
+def device_at(turn):
+    place = turn >> 3
+    x = ((turn >> 1) & 3) ^ ((place & 1) * 3)
+    y = (RING_Y >> (place * 2)) & 3
+    z = (RING_Z >> (place * 2)) & 3
+    return z * 32 + y * 8 + x * 2 + (turn & 1)
+
+
 def pack_kernel(
     emb_ref, cluster_ref, rank_ref, out_ref, place_ref, raw, unit, left, right, arrived
 ):
@@ -76,39 +88,46 @@
     which = iota((N, ROWS), 0)
     at_home = which == home
     at_home_b = flag(at_home)
+    row, column = iota((N, N), 0), iota((N, N), 1)
+    upper = flag(row < column)
     count = dot_nt(jnp.ones((8, ROWS), BF16), at_home_b)
     chunks = jnp.concatenate([at_home_b[:, c * 128 : (c + 1) * 128] for c in range(8)], axis=0)
-    lower = flag(iota((128, 128), 0) <= iota((128, 128), 1))
-    running = dot(chunks, jnp.concatenate([lower, jnp.ones((128, 128), BF16)], axis=1))
-
-    window = count - float(SLOTS)
-    queue = jnp.maximum(window, 0.0)
-    for step in (1, 2, 4, 8, 16, 32, 64):
-        queue = jnp.maximum(queue, window + pltpu.roll(queue, step, 1))
-        window = window + pltpu.roll(window, step, 1)
-    ahead = pltpu.roll(queue, 1, 1)
-    ahead_high = jnp.floor(ahead * (1.0 / 256.0)) * 256.0
-    ahead = dot(jnp.concatenate([ahead_high, ahead - ahead_high], axis=0).astype(BF16), at_home_b)
-    ahead = ahead[0:1] + ahead[8:9]
-
-    before = jnp.zeros((128, 128), F32)
+    running = dot(chunks, jnp.concatenate([upper, jnp.ones((N, N), BF16)], axis=1))
+    totals = [running[c * 128 : (c + 1) * 128, 128:] for c in range(8)]
+    total = sum(totals[1:], totals[0])
+
+    over = total - float(SLOTS)
+    below = dot(flag(row > column), over.astype(BF16))
+    along = dot((count - float(SLOTS)).astype(BF16), upper)
+    round_trip = float(ROWS - SLOTS * N)
+    ahead = below + jnp.max(
+        jnp.where(column < row, 0.0, round_trip) - along[:1], axis=1, keepdims=True
+    )
+    ahead = jnp.maximum(ahead, 0.0)
+    queue = along[:1] + count[:1] - float(SLOTS)
+    queue = queue + jnp.max(
+        jnp.where(row <= column, 0.0, round_trip) - below, axis=0, keepdims=True
+    )
+    queue = jnp.maximum(queue, 0.0)
+
+    before = ahead
     turn = []
     for c in range(8):
-        part = running[c * 128 : (c + 1) * 128]
+        part = running[c * 128 : (c + 1) * 128, :128]
         turn.append(
             jnp.sum(
-                jnp.where(at_home[:, c * 128 : (c + 1) * 128], part[:, :128] + before, 0.0),
+                jnp.where(at_home[:, c * 128 : (c + 1) * 128], part + before, 0.0),
                 axis=0,
                 keepdims=True,
             )
         )
-        before = before + part[:, 128:]
-    offset = jnp.concatenate(turn, axis=1) - 1.0 + ahead
+        before = before + totals[c]
+    offset = jnp.concatenate(turn, axis=1)
     hops = jnp.floor((offset + 0.5) * (1.0 / SLOTS))
     slot = (offset - hops * SLOTS).astype(I32)
     hops = hops.astype(I32)
-    target = (home + hops) & (N - 1)
-    place_ref[0:1, :] = home
+    target = device_at((home + hops) & (N - 1))
+    place_ref[0:1, :] = device_at(home)
     place_ref[1:2, :] = jnp.minimum(hops, 7) * 16 + slot
 
     for c in range(4):
@@ -134,7 +153,7 @@
     value = jnp.where((iota((META, ROWS), 0) & 15) == slot, value, 0)
     meta = dot_nt(flag(which == target), value.astype(F32).astype(BF16))
     left[pl.ds(6, N, stride=8), :] = meta
-    right[pl.ds(6, N, stride=8), :] = jnp.broadcast_to(jnp.minimum(queue[:1], 255.0), (N, 128))
+    right[pl.ds(6, N, stride=8), :] = jnp.broadcast_to(jnp.minimum(queue, 255.0), (N, 128))
     left[pl.ds(7, N, stride=8), :] = jnp.zeros((N, 128), F32)
     right[pl.ds(7, N, stride=8), :] = jnp.zeros((N, 128), F32)
     extra_row = jnp.where(slot >= 8, (slot - 8) * N + target, -1)
@@ -413,6 +432,11 @@
     return lax.ppermute(array, "dev", [(i, (i + by) % N) for i in range(N)])
 
 
+def moved_back(array, by):
+    pairs = [(device_at(i), device_at((i - by) % N)) for i in range(N)]
+    return lax.ppermute(array, "dev", pairs)
+
+
 def swapped(array):
     return lax.all_to_all(array, "dev", split_axis=0, concat_axis=0, tiled=True)
 
@@ -463,8 +487,8 @@
     packed, place = pack(emb, cluster, rank)
     got = swapped(packed.reshape(N, 8, D + 256)).reshape(MAIN, D + 256)
     late, meta, near, far, bad = unpack(got)
-    near = passed_along(near, -1)
-    far = passed_along(far, -2)
+    near = moved_back(near, 1)
+    far = moved_back(far, 2)
     row, best = local_best(got, late, meta)
     answers = cross_best(got, late, row, best, near, far)
     back = swapped(answers.reshape(N, 1, N)).reshape(N, N)

time: 76 us -> 71.7 us (0.943)
  starting transfers between devices: 10.8 us -> 5.41 us
  waiting for transfers between devices: 9.66 us -> 10.8 us
    all_to_all x1, starting transfers between devices: 8.79 us -> 4.41 us  [swapped(): return lax.all_to_all(array, 'dev', split_axis=0, concat_axis=0, tiled=True)]
    ppermute x2, starting transfers between devices: 1.96 us -> 1 us  [moved_back(): return lax.ppermute(array, 'dev', pairs)]
    ppermute x2, waiting for transfers between devices: 0.7 us -> 1.66 us  [moved_back(): return lax.ppermute(array, 'dev', pairs)]
where the time goes in v3:
time: 71.7 us; the launch traced here: 71.5 us
  blocking collectives  41.8 us (58%)
  Pallas kernels  11.9 us (17%)
  waiting for transfers between devices  10.8 us (15%)
  starting transfers between devices  5.41 us (8%)
  between operations  0.76 us (1%)
    all_to_all x1, blocking collectives, swapped(): return lax.all_to_all(array, 'dev', split_axis=0, concat_axis=0, tiled=True)  41.8 us
    all_to_all x1, waiting for transfers between devices, swapped(): return lax.all_to_all(array, 'dev', split_axis=0, concat_axis=0, tiled=True)  9.1 us
    pallas_call x1, Pallas kernels, pack(): pl.pallas_call(pack_kernel, in_specs=[pl.BlockSpec(memory_space=pl.ANY),...  4.82 us
    all_to_all x1, starting transfers between devices, swapped(): return lax.all_to_all(array, 'dev', split_axis=0, concat_axis=0, tiled=True)  4.41 us
    pallas_call x1, Pallas kernels, local_best(): pl.pallas_call(local_kernel, out_shape=(jax.ShapeDtypeStruct((16, ALL), F...  3.42 us
    pallas_call x1, Pallas kernels, cross_best(): pl.pallas_call(cross_kernel, out_shape=jax.ShapeDtypeStruct((N, N), F32),...  1.82 us
    ppermute x2, waiting for transfers between devices, moved_back(): return lax.ppermute(array, 'dev', pairs)  1.66 us
    pallas_call x1, Pallas kernels, unpack(): pl.pallas_call(unpack_kernel, out_shape=(jax.ShapeDtypeStruct((EXTRA, D),...  1.55 us
  transfers between devices with their start and end apart: 3, of which 2 were waited for; matrix products, arithmetic and copies ran while one was open for 0% of the time, Pallas kernels for 5%

profile of v3, /device:TPU:1, one launch (start us, length us, event | category | flops | bytes accessed | tf_op | source)
XLA Modules:
  0.0 71.5 jit_solution(8084400548226571491)
XLA Ops:
  0.0 4.8 %pack.1 = (bf16[1024,1024]{1,0:T(8,128)(2,1)S(1)}, s32[2,1024]{1,0:T(2,128)S(1)}) custom-call(bf16[1024,768]{1,0:T(8,128)(2,1)} %emb_ref.1, s32[1,1024]{1,0:T(1,128)} %bitcast.100, s32[1,1024]{1,0:T(1,128)} %bitcast.101), custom_call_target="tpu_custom_call" | custom-call | tf_op jit(solution)/shard_map/pack/pallas_call | solution.py:176
  4.8 41.8 %all_to_all.45 = bf16[128,8,1024]{2,1,0:T(8,128)(2,1)S(1)} all-to-all(bf16[128,8,1024]{2,1,0:T(8,128)(2,1)S(1)} %bitcast.84), channel_id=1, replica_groups=mesh['dev'=128] {'dev'}, dimensions={0} | all-to-all | bytes 4194304 | tf_op jit(solution)/shard_map/all_to_all | solution.py:441
  46.7 1.6 %unpack.1 = (bf16[256,768]{1,0:T(8,128)(2,1)S(1)}, f32[128,128]{1,0:T(8,128)S(1)}, bf16[144,896]{1,0:T(8,128)(2,1)S(1)}, bf16[16,896]{1,0:T(8,128)(2,1)S(1)}, s32[1,1]{1,0:T(1,128)}) custom-call(bf16[1024,1024]{1,0:T(8,128)(2,1)S(1)} %bitcast.81), custom_call_target="tpu_custom_call" | custom-call | tf_op jit(solution)/shard_map/unpack/pallas_call | solution.py:266
  48.2 1.0 %collective-permute-start.6 = (bf16[144,896]{1,0:T(8,128)(2,1)S(1)}, bf16[144,896]{1,0:T(8,128)(2,1)S(1)}, u32[]{:S(2)}, u32[]{:S(2)}) collective-permute-start(bf16[144,896]{1,0:T(8,128)(2,1)S(1)} %get-tuple-element.161), channel_id=1, source_target_pairs={{0,9},{1,0},{2,1},{3,2},{4,3},{5,4},{6,5},{7,6},{38,7},{39,38},{36... | collective-permute-start | bytes 774152 | tf_op jit(solution)/shard_map/ppermute | solution.py:437
  49.2 0.0 collective-permute-start.7
  49.2 3.4 %local_best.1 = (f32[16,1280]{1,0:T(8,128)S(1)}, f32[8,1280]{1,0:T(8,128)S(1)}) custom-call(bf16[1024,1024]{1,0:T(8,128)(2,1)S(1)} %bitcast.82, bf16[256,768]{1,0:T(8,128)(2,1)S(1)} %get-tuple-element.157.late_ref, f32[128,128]{1,0:T(8,128)S(1)} %get-tuple-element.158.meta_ref), custom_call_target="tpu_custom_call" | custom-call | flops 2516582400 | bytes 3932160 | tf_op jit(solution)/shard_map/local_best/pallas_call | solution.py:327
  52.6 0.0 copy-start
  52.7 0.0 copy-start.1
  52.7 0.0 copy-start.2
  52.7 0.0 collective-permute-done.7.far_ref
  52.7 1.7 %collective-permute-done.6.near_ref = bf16[144,896]{1,0:T(8,128)(2,1)S(1)} collective-permute-done((bf16[144,896]{1,0:T(8,128)(2,1)S(1)}, bf16[144,896]{1,0:T(8,128)(2,1)S(1)}, u32[]{:S(2)}, u32[]{:S(2)}) %collective-permute-start.6) | collective-permute-done | bytes 258080 | tf_op jit(solution)/shard_map/ppermute | solution.py:437
  54.3 1.8 %cross_best.1 = f32[128,128]{1,0:T(8,128)} custom-call(bf16[1024,1024]{1,0:T(8,128)(2,1)S(1)} %bitcast.83, bf16[256,768]{1,0:T(8,128)(2,1)S(1)} %get-tuple-element.157.late_ref, f32[16,1280]{1,0:T(8,128)S(1)} %get-tuple-element.159.row_ref, f32[8,1280]{1,0:T(8,128)S(1)} %get-tuple-element.160.best_ref, bf16[144,896]{1,0:T(8,128)(2,1)S(1)} %collective-permute-done.6.near_ref, ...), custom_call_target="tpu_custom_call" | custom-call | tf_op jit(solution)/shard_map/cross_best/pallas_call | solution.py:403
  56.2 4.4 %all-to-all-start.5 = ((f32[128,1,128]{2,1,0:T(1,128)}), f32[128,1,128]{2,1,0:T(1,128)S(1)}, u32[]{:S(2)}, u32[]{:S(2)}) async-start(f32[128,1,128]{2,1,0:T(1,128)} %bitcast.29), calls=%async_computation.5 | async-start | bytes 131072 | tf_op jit(solution)/shard_map/all_to_all | solution.py:441
  61.2 9.1 %all-to-all-done.5 = f32[128,1,128]{2,1,0:T(1,128)S(1)} async-done(((f32[128,1,128]{2,1,0:T(1,128)}), f32[128,1,128]{2,1,0:T(1,128)S(1)}, u32[]{:S(2)}, u32[]{:S(2)}) %all-to-all-start.5) | async-done | bytes 65568 | tf_op jit(solution)/shard_map/all_to_all | solution.py:441
  70.3 0.3 pick.1
  70.6 0.0 copy-done
  70.7 0.0 copy-done.1
  70.7 0.0 copy-done.2
  70.7 0.2 conditional.1
  70.9 0.0 copy-start.3
  70.9 0.6 copy-done.3
Async XLA Ops:
  48.2 6.1 %collective-permute-start.6 = (bf16[144,896]{1,0:T(8,128)(2,1)S(1)}, bf16[144,896]{1,0:T(8,128)(2,1)S(1)}, u32[]{:S(2)}, u32[]{:S(2)}) collective-permute-start(bf16[144,896]{1,0:T(8,128)(2,1)S(1)} %get-tuple-element.161), channel_id=1, source_target_pairs={{0,9},{1,0},{2,1},{3,2},{4,3},{5,4},{6,5},{7,6},{38,7},{39,38},{36... | collective-permute-start | bytes 774152 | tf_op jit(solution)/shard_map/ppermute | solution.py:437
  49.2 3.5 %collective-permute-start.7 = (bf16[16,896]{1,0:T(8,128)(2,1)S(1)}, bf16[16,896]{1,0:T(8,128)(2,1)S(1)}, u32[]{:S(2)}, u32[]{:S(2)}) collective-permute-start(bf16[16,896]{1,0:T(8,128)(2,1)S(1)} %get-tuple-element.162), channel_id=1, source_target_pairs={{0,8},{1,9},{2,0},{3,1},{4,2},{5,3},{6,4},{7,5},{38,6},{39,7},{36,... | collective-permute-start | bytes 86024 | tf_op jit(solution)/shard_map/ppermute | solution.py:437
  52.6 18.0 %copy-start = (bf16[1024,768]{1,0:T(8,128)(2,1)S(1)}, bf16[1024,768]{1,0:T(8,128)(2,1)}, u32[]{:S(2)}) copy-start(bf16[1024,768]{1,0:T(8,128)(2,1)} %emb_ref.1) | copy-start | bytes 4718596
  52.7 18.0 %copy-start.1 = (s32[1024]{0:T(1024)S(1)}, s32[1024]{0:T(1024)}, u32[]{:S(2)}) copy-start(s32[1024]{0:T(1024)} %param.12) | copy-start | bytes 12292
  52.7 18.0 %copy-start.2 = (s32[1024]{0:T(1024)S(1)}, s32[1024]{0:T(1024)}, u32[]{:S(2)}) copy-start(s32[1024]{0:T(1024)} %param.13) | copy-start | bytes 12292
  56.2 14.2 %all-to-all-start.5 = ((f32[128,1,128]{2,1,0:T(1,128)}), f32[128,1,128]{2,1,0:T(1,128)S(1)}, u32[]{:S(2)}, u32[]{:S(2)}) async-start(f32[128,1,128]{2,1,0:T(1,128)} %bitcast.29), calls=%async_computation.5 | async-start | bytes 131072 | tf_op jit(solution)/shard_map/all_to_all | solution.py:441
  70.9 0.6 copy-start.3

commit v4 on v3

--- a/solution.py
+++ b/solution.py
@@ -1,5 +1,3 @@
-import functools
-
 import jax
 import jax.numpy as jnp
 from jax import lax
@@ -69,19 +67,20 @@
 
 
 def pack_kernel(
-    emb_ref, cluster_ref, rank_ref, out_ref, place_ref, raw, unit, left, right, arrived
+    emb_ref, cluster_ref, rank_ref, out_ref, place_ref, raw, ids, left, right, arrived
 ):
     loads = [
-        pltpu.make_async_copy(
-            emb_ref.at[pl.ds(c * 256, 256), :], raw.at[pl.ds(c * 256, 256), :], arrived.at[c]
-        )
-        for c in range(4)
+        pltpu.make_async_copy(cluster_ref, ids.at[0], arrived.at[0]),
+        pltpu.make_async_copy(rank_ref, ids.at[1], arrived.at[1]),
+        pltpu.make_async_copy(emb_ref, raw, arrived.at[2]),
     ]
     for load in loads:
         load.start()
 
-    cluster = cluster_ref[...]
-    rank = rank_ref[...]
+    loads[0].wait()
+    cluster = ids[0]
+    loads[1].wait()
+    rank = ids[1]
     home = cluster & (N - 1)
     member = cluster // N
 
@@ -130,11 +129,11 @@
     place_ref[0:1, :] = device_at(home)
     place_ref[1:2, :] = jnp.minimum(hops, 7) * 16 + slot
 
-    for c in range(4):
-        loads[c].wait()
-        wide = raw[c * 256 : (c + 1) * 256, :].astype(F32)
-        scale = lax.rsqrt(jnp.sum(wide * wide, axis=-1, keepdims=True) + 1e-06)
-        unit[c * 256 : (c + 1) * 256, :] = (wide * scale).astype(BF16)
+    loads[2].wait()
+
+    def unit_rows(chosen):
+        wide = dot(chosen, raw[...])
+        return wide * lax.rsqrt(jnp.sum(wide * wide, axis=-1, keepdims=True) + 1e-06)
 
     def spread(value):
         return jnp.broadcast_to(value, (16, ROWS))
@@ -157,7 +156,7 @@
     left[pl.ds(7, N, stride=8), :] = jnp.zeros((N, 128), F32)
     right[pl.ds(7, N, stride=8), :] = jnp.zeros((N, 128), F32)
     extra_row = jnp.where(slot >= 8, (slot - 8) * N + target, -1)
-    late = dot(flag(iota((EXTRA, ROWS), 0) == extra_row), unit[...])
+    late = unit_rows(flag(iota((EXTRA, ROWS), 0) == extra_row))
     for k in range(2):
         for piece in range(3):
             rows = late[k * N : (k + 1) * N, piece * 256 : (piece + 1) * 256]
@@ -169,27 +168,23 @@
     main_row = jnp.where(slot < 8, target * 8 + slot, -1)
     for b in range(4):
         chosen = flag(iota((256, ROWS), 0) == main_row - b * 256)
-        out_ref[b * 256 : (b + 1) * 256, :D] = dot(chosen, unit[...]).astype(BF16)
+        out_ref[b * 256 : (b + 1) * 256, :D] = unit_rows(chosen).astype(BF16)
 
 
 def pack(emb, cluster, rank):
     return pl.pallas_call(
         pack_kernel,
-        in_specs=[
-            pl.BlockSpec(memory_space=pl.ANY),
-            pl.BlockSpec(memory_space=pltpu.VMEM),
-            pl.BlockSpec(memory_space=pltpu.VMEM),
-        ],
+        in_specs=[pl.BlockSpec(memory_space=pl.ANY)] * 3,
         out_shape=(
             jax.ShapeDtypeStruct((MAIN, D + 256), BF16),
             jax.ShapeDtypeStruct((2, ROWS), I32),
         ),
         scratch_shapes=[
             pltpu.VMEM((ROWS, D), BF16),
-            pltpu.VMEM((ROWS, D), BF16),
+            pltpu.VMEM((2, 1, ROWS), I32),
             pltpu.VMEM((MAIN, 128), F32),
             pltpu.VMEM((MAIN, 128), F32),
-            pltpu.SemaphoreType.DMA((4,)),
+            pltpu.SemaphoreType.DMA((3,)),
         ],
         compiler_params=LIMIT,
         name="pack",

time: 71.7 us -> 71 us (level)
  no operation moved by 1% of the time
where the time goes in v4:
time: 71 us; the launch traced here: 70.8 us
  blocking collectives  41.8 us (59%)
  Pallas kernels  11.2 us (16%)
  waiting for transfers between devices  10.8 us (15%)
  starting transfers between devices  5.41 us (8%)
  between operations  0.76 us (1%)
    all_to_all x1, blocking collectives, swapped(): return lax.all_to_all(array, 'dev', split_axis=0, concat_axis=0, tiled=True)  41.8 us
    all_to_all x1, waiting for transfers between devices, swapped(): return lax.all_to_all(array, 'dev', split_axis=0, concat_axis=0, tiled=True)  9.1 us
    all_to_all x1, starting transfers between devices, swapped(): return lax.all_to_all(array, 'dev', split_axis=0, concat_axis=0, tiled=True)  4.41 us
    pallas_call x1, Pallas kernels, pack(): pl.pallas_call(pack_kernel, in_specs=[pl.BlockSpec(memory_space=pl.ANY)]...  4.13 us
    pallas_call x1, Pallas kernels, local_best(): pl.pallas_call(local_kernel, out_shape=(jax.ShapeDtypeStruct((16, ALL), F...  3.42 us
    pallas_call x1, Pallas kernels, cross_best(): pl.pallas_call(cross_kernel, out_shape=jax.ShapeDtypeStruct((N, N), F32),...  1.82 us
    ppermute x2, waiting for transfers between devices, moved_back(): return lax.ppermute(array, 'dev', pairs)  1.66 us
    pallas_call x1, Pallas kernels, unpack(): pl.pallas_call(unpack_kernel, out_shape=(jax.ShapeDtypeStruct((EXTRA, D),...  1.56 us
  transfers between devices with their start and end apart: 3, of which 2 were waited for; matrix products, arithmetic and copies ran while one was open for 0% of the time, Pallas kernels for 5%

profile of v4, /device:TPU:1, one launch (start us, length us, event | category | flops | bytes accessed | tf_op | source)
XLA Modules:
  0.0 70.8 jit_solution(6362700645708186873)
XLA Ops:
  0.0 4.1 %pack.1 = (bf16[1024,1024]{1,0:T(8,128)(2,1)S(1)}, s32[2,1024]{1,0:T(2,128)S(1)}) custom-call(bf16[1024,768]{1,0:T(8,128)(2,1)} %emb_ref.1, s32[1,1024]{1,0:T(1,128)} %bitcast.100, s32[1,1024]{1,0:T(1,128)} %bitcast.101), custom_call_target="tpu_custom_call" | custom-call | tf_op jit(solution)/shard_map/pack/pallas_call | solution.py:175
  4.1 41.8 %all_to_all.45 = bf16[128,8,1024]{2,1,0:T(8,128)(2,1)S(1)} all-to-all(bf16[128,8,1024]{2,1,0:T(8,128)(2,1)S(1)} %bitcast.84), channel_id=1, replica_groups=mesh['dev'=128] {'dev'}, dimensions={0} | all-to-all | bytes 4194304 | tf_op jit(solution)/shard_map/all_to_all | solution.py:436
  46.0 1.6 %unpack.1 = (bf16[256,768]{1,0:T(8,128)(2,1)S(1)}, f32[128,128]{1,0:T(8,128)S(1)}, bf16[144,896]{1,0:T(8,128)(2,1)S(1)}, bf16[16,896]{1,0:T(8,128)(2,1)S(1)}, s32[1,1]{1,0:T(1,128)}) custom-call(bf16[1024,1024]{1,0:T(8,128)(2,1)S(1)} %bitcast.81), custom_call_target="tpu_custom_call" | custom-call | tf_op jit(solution)/shard_map/unpack/pallas_call | solution.py:261
  47.5 1.0 %collective-permute-start.6 = (bf16[144,896]{1,0:T(8,128)(2,1)S(1)}, bf16[144,896]{1,0:T(8,128)(2,1)S(1)}, u32[]{:S(2)}, u32[]{:S(2)}) collective-permute-start(bf16[144,896]{1,0:T(8,128)(2,1)S(1)} %get-tuple-element.161), channel_id=1, source_target_pairs={{0,9},{1,0},{2,1},{3,2},{4,3},{5,4},{6,5},{7,6},{38,7},{39,38},{36... | collective-permute-start | bytes 774152 | tf_op jit(solution)/shard_map/ppermute | solution.py:432
  48.5 0.0 collective-permute-start.7
  48.5 3.4 %local_best.1 = (f32[16,1280]{1,0:T(8,128)S(1)}, f32[8,1280]{1,0:T(8,128)S(1)}) custom-call(bf16[1024,1024]{1,0:T(8,128)(2,1)S(1)} %bitcast.82, bf16[256,768]{1,0:T(8,128)(2,1)S(1)} %get-tuple-element.157.late_ref, f32[128,128]{1,0:T(8,128)S(1)} %get-tuple-element.158.meta_ref), custom_call_target="tpu_custom_call" | custom-call | flops 2516582400 | bytes 3932160 | tf_op jit(solution)/shard_map/local_best/pallas_call | solution.py:322
  52.0 0.0 copy-start
  52.0 0.0 copy-start.1
  52.0 0.0 copy-start.2
  52.0 0.0 collective-permute-done.7.far_ref
  52.0 1.7 %collective-permute-done.6.near_ref = bf16[144,896]{1,0:T(8,128)(2,1)S(1)} collective-permute-done((bf16[144,896]{1,0:T(8,128)(2,1)S(1)}, bf16[144,896]{1,0:T(8,128)(2,1)S(1)}, u32[]{:S(2)}, u32[]{:S(2)}) %collective-permute-start.6) | collective-permute-done | bytes 258080 | tf_op jit(solution)/shard_map/ppermute | solution.py:432
  53.7 1.8 %cross_best.1 = f32[128,128]{1,0:T(8,128)} custom-call(bf16[1024,1024]{1,0:T(8,128)(2,1)S(1)} %bitcast.83, bf16[256,768]{1,0:T(8,128)(2,1)S(1)} %get-tuple-element.157.late_ref, f32[16,1280]{1,0:T(8,128)S(1)} %get-tuple-element.159.row_ref, f32[8,1280]{1,0:T(8,128)S(1)} %get-tuple-element.160.best_ref, bf16[144,896]{1,0:T(8,128)(2,1)S(1)} %collective-permute-done.6.near_ref, ...), custom_call_target="tpu_custom_call" | custom-call | tf_op jit(solution)/shard_map/cross_best/pallas_call | solution.py:398
  55.5 4.4 %all-to-all-start.5 = ((f32[128,1,128]{2,1,0:T(1,128)}), f32[128,1,128]{2,1,0:T(1,128)S(1)}, u32[]{:S(2)}, u32[]{:S(2)}) async-start(f32[128,1,128]{2,1,0:T(1,128)} %bitcast.29), calls=%async_computation.5 | async-start | bytes 131072 | tf_op jit(solution)/shard_map/all_to_all | solution.py:436
  60.5 9.1 %all-to-all-done.5 = f32[128,1,128]{2,1,0:T(1,128)S(1)} async-done(((f32[128,1,128]{2,1,0:T(1,128)}), f32[128,1,128]{2,1,0:T(1,128)S(1)}, u32[]{:S(2)}, u32[]{:S(2)}) %all-to-all-start.5) | async-done | bytes 65568 | tf_op jit(solution)/shard_map/all_to_all | solution.py:436
  69.6 0.3 pick.1
  70.0 0.0 copy-done
  70.0 0.0 copy-done.1
  70.0 0.0 copy-done.2
  70.0 0.2 conditional.1
  70.2 0.0 copy-start.3
  70.2 0.6 copy-done.3
Async XLA Ops:
  47.5 6.1 %collective-permute-start.6 = (bf16[144,896]{1,0:T(8,128)(2,1)S(1)}, bf16[144,896]{1,0:T(8,128)(2,1)S(1)}, u32[]{:S(2)}, u32[]{:S(2)}) collective-permute-start(bf16[144,896]{1,0:T(8,128)(2,1)S(1)} %get-tuple-element.161), channel_id=1, source_target_pairs={{0,9},{1,0},{2,1},{3,2},{4,3},{5,4},{6,5},{7,6},{38,7},{39,38},{36... | collective-permute-start | bytes 774152 | tf_op jit(solution)/shard_map/ppermute | solution.py:432
  48.5 3.5 %collective-permute-start.7 = (bf16[16,896]{1,0:T(8,128)(2,1)S(1)}, bf16[16,896]{1,0:T(8,128)(2,1)S(1)}, u32[]{:S(2)}, u32[]{:S(2)}) collective-permute-start(bf16[16,896]{1,0:T(8,128)(2,1)S(1)} %get-tuple-element.162), channel_id=1, source_target_pairs={{0,8},{1,9},{2,0},{3,1},{4,2},{5,3},{6,4},{7,5},{38,6},{39,7},{36,... | collective-permute-start | bytes 86024 | tf_op jit(solution)/shard_map/ppermute | solution.py:432
  52.0 18.0 %copy-start = (bf16[1024,768]{1,0:T(8,128)(2,1)S(1)}, bf16[1024,768]{1,0:T(8,128)(2,1)}, u32[]{:S(2)}) copy-start(bf16[1024,768]{1,0:T(8,128)(2,1)} %emb_ref.1) | copy-start | bytes 4718596
  52.0 18.0 %copy-start.1 = (s32[1024]{0:T(1024)S(1)}, s32[1024]{0:T(1024)}, u32[]{:S(2)}) copy-start(s32[1024]{0:T(1024)} %param.12) | copy-start | bytes 12292
  52.0 18.0 %copy-start.2 = (s32[1024]{0:T(1024)S(1)}, s32[1024]{0:T(1024)}, u32[]{:S(2)}) copy-start(s32[1024]{0:T(1024)} %param.13) | copy-start | bytes 12292
  55.5 14.2 %all-to-all-start.5 = ((f32[128,1,128]{2,1,0:T(1,128)}), f32[128,1,128]{2,1,0:T(1,128)S(1)}, u32[]{:S(2)}, u32[]{:S(2)}) async-start(f32[128,1,128]{2,1,0:T(1,128)} %bitcast.29), calls=%async_computation.5 | async-start | bytes 131072 | tf_op jit(solution)/shard_map/all_to_all | solution.py:436
  70.2 0.6 copy-start.3

commit v5 on v4

--- a/solution.py
+++ b/solution.py
@@ -485,11 +485,15 @@
     near = moved_back(near, 1)
     far = moved_back(far, 2)
     row, best = local_best(got, late, meta)
+    row, bad = lax.optimization_barrier((row, bad))
+    slow = bad[0, 0] > 0
+    row, slow = lax.optimization_barrier((row, slow))
     answers = cross_best(got, late, row, best, near, far)
     back = swapped(answers.reshape(N, 1, N)).reshape(N, N)
+    back, slow, emb, cluster, rank = lax.optimization_barrier((back, slow, emb, cluster, rank))
     nearest = pick(back, place).reshape(ROWS)
     return lax.cond(
-        bad[0, 0] > 0,
+        slow,
         by_pools,
         lambda emb, cluster, rank: nearest,
         emb,

time: 71 us -> 69.8 us (0.983)
  blocking collectives: 41.8 us -> 55.4 us
  waiting for transfers between devices: 10.8 us -> 0.9 us
  starting transfers between devices: 5.41 us -> 1 us
    all_to_all x1 -> x2, blocking collectives: 41.8 us -> 55.4 us  [swapped(): return lax.all_to_all(array, 'dev', split_axis=0, concat_axis=0, tiled=True)]
    all_to_all x1 -> x0, waiting for transfers between devices: 9.1 us -> none  [swapped(): return lax.all_to_all(array, 'dev', split_axis=0, concat_axis=0, tiled=True)]
    all_to_all x1 -> x0, starting transfers between devices: 4.41 us -> none  [swapped(): return lax.all_to_all(array, 'dev', split_axis=0, concat_axis=0, tiled=True)]
    ppermute x2, waiting for transfers between devices: 1.66 us -> 0.9 us  [moved_back(): return lax.ppermute(array, 'dev', pairs)]
  transfers between devices with their start and end apart: 3 -> 2, of which waited for: 2 -> 1; matrix products, arithmetic and copies ran while one was open for 0% -> 0% of each run, Pallas kernels for 5% -> 5%
where the time goes in v5:
time: 69.8 us; the launch traced here: 69.6 us
  blocking collectives  55.4 us (79%)
  Pallas kernels  10.6 us (15%)
  starting transfers between devices  1 us (1%)
  waiting for transfers between devices  0.9 us (1%)
  between operations  0.87 us (1%)
    all_to_all x2, blocking collectives, swapped(): return lax.all_to_all(array, 'dev', split_axis=0, concat_axis=0, tiled=True)  55.4 us
    pallas_call x1, Pallas kernels, pack(): pl.pallas_call(pack_kernel, in_specs=[pl.BlockSpec(memory_space=pl.ANY)]...  4.13 us
    pallas_call x1, Pallas kernels, local_best(): pl.pallas_call(local_kernel, out_shape=(jax.ShapeDtypeStruct((16, ALL), F...  3.42 us
    pallas_call x1, Pallas kernels, unpack(): pl.pallas_call(unpack_kernel, out_shape=(jax.ShapeDtypeStruct((EXTRA, D),...  1.56 us
  transfers between devices with their start and end apart: 2, of which 1 were waited for; matrix products, arithmetic and copies ran while one was open for 0% of the time, Pallas kernels for 5%

profile of v5, /device:TPU:1, one launch (start us, length us, event | category | flops | bytes accessed | tf_op | source)
XLA Modules:
  0.0 69.6 jit_solution(260047354813117991)
XLA Ops:
  0.0 4.1 %pack.1 = (bf16[1024,1024]{1,0:T(8,128)(2,1)S(1)}, s32[2,1024]{1,0:T(2,128)S(1)}) custom-call(bf16[1024,768]{1,0:T(8,128)(2,1)} %emb_ref.1, s32[1,1024]{1,0:T(1,128)} %bitcast.101, s32[1,1024]{1,0:T(1,128)} %bitcast.102), custom_call_target="tpu_custom_call" | custom-call | tf_op jit(solution)/shard_map/pack/pallas_call | solution.py:175
  4.1 41.8 %all_to_all.45 = bf16[128,8,1024]{2,1,0:T(8,128)(2,1)S(1)} all-to-all(bf16[128,8,1024]{2,1,0:T(8,128)(2,1)S(1)} %bitcast.84), channel_id=1, replica_groups=mesh['dev'=128] {'dev'}, dimensions={0} | all-to-all | bytes 4194304 | tf_op jit(solution)/shard_map/all_to_all | solution.py:436
  46.0 1.6 %unpack.1 = (bf16[256,768]{1,0:T(8,128)(2,1)S(1)}, f32[128,128]{1,0:T(8,128)S(1)}, bf16[144,896]{1,0:T(8,128)(2,1)S(1)}, bf16[16,896]{1,0:T(8,128)(2,1)S(1)}, s32[1,1]{1,0:T(1,128)}) custom-call(bf16[1024,1024]{1,0:T(8,128)(2,1)S(1)} %bitcast.81), custom_call_target="tpu_custom_call" | custom-call | tf_op jit(solution)/shard_map/unpack/pallas_call | solution.py:261
  47.5 1.0 %collective-permute-start.6 = (bf16[144,896]{1,0:T(8,128)(2,1)S(1)}, bf16[144,896]{1,0:T(8,128)(2,1)S(1)}, u32[]{:S(2)}, u32[]{:S(2)}) collective-permute-start(bf16[144,896]{1,0:T(8,128)(2,1)S(1)} %get-tuple-element.173), channel_id=1, source_target_pairs={{0,9},{1,0},{2,1},{3,2},{4,3},{5,4},{6,5},{7,6},{38,7},{39,38},{36... | collective-permute-start | bytes 774152 | tf_op jit(solution)/shard_map/ppermute | solution.py:432
  48.5 0.0 collective-permute-start.7
  48.5 3.4 %local_best.1 = (f32[16,1280]{1,0:T(8,128)S(1)}, f32[8,1280]{1,0:T(8,128)S(1)}) custom-call(bf16[1024,1024]{1,0:T(8,128)(2,1)S(1)} %bitcast.82, bf16[256,768]{1,0:T(8,128)(2,1)S(1)} %get-tuple-element.165.late_ref, f32[128,128]{1,0:T(8,128)S(1)} %get-tuple-element.166.meta_ref), custom_call_target="tpu_custom_call" | custom-call | flops 2516582400 | bytes 3932160 | tf_op jit(solution)/shard_map/local_best/pallas_call | solution.py:322
  52.0 0.0 copy-start
  52.0 0.0 copy-start.1
  52.0 0.0 copy-start.2
  52.8 0.0 collective-permute-done.7.far_ref
  52.8 0.9 %collective-permute-done.6.near_ref = bf16[144,896]{1,0:T(8,128)(2,1)S(1)} collective-permute-done((bf16[144,896]{1,0:T(8,128)(2,1)S(1)}, bf16[144,896]{1,0:T(8,128)(2,1)S(1)}, u32[]{:S(2)}, u32[]{:S(2)}) %collective-permute-start.6) | collective-permute-done | bytes 258080 | tf_op jit(solution)/shard_map/ppermute | solution.py:432
  53.7 1.2 %cross_best.1 = f32[128,128]{1,0:T(8,128)S(1)} custom-call(bf16[1024,1024]{1,0:T(8,128)(2,1)S(1)} %bitcast.83, bf16[256,768]{1,0:T(8,128)(2,1)S(1)} %get-tuple-element.165.late_ref, f32[16,1280]{1,0:T(8,128)S(1)} %get-tuple-element.171.row_ref, f32[8,1280]{1,0:T(8,128)S(1)} %get-tuple-element.172.best_ref, ...), custom_call_target="tpu_custom_call" | custom-call | tf_op jit(solution)/shard_map/cross_best/pallas_call | solution.py:398
  54.9 13.6 %all_to_all.46 = f32[128,1,128]{2,1,0:T(1,128)S(1)} all-to-all(f32[128,1,128]{2,1,0:T(1,128)S(1)} %bitcast.85), channel_id=1, replica_groups=mesh['dev'=128] {'dev'}, dimensions={0} | all-to-all | bytes 131072 | tf_op jit(solution)/shard_map/all_to_all | solution.py:436
  68.4 0.3 pick.1
  68.7 0.0 copy-done
  68.7 0.0 copy-done.1
  68.8 0.0 copy-done.2
  68.8 0.2 conditional.1
  69.0 0.0 copy-start.3
  69.0 0.6 copy-done.3
Async XLA Ops:
  47.5 6.1 %collective-permute-start.6 = (bf16[144,896]{1,0:T(8,128)(2,1)S(1)}, bf16[144,896]{1,0:T(8,128)(2,1)S(1)}, u32[]{:S(2)}, u32[]{:S(2)}) collective-permute-start(bf16[144,896]{1,0:T(8,128)(2,1)S(1)} %get-tuple-element.173), channel_id=1, source_target_pairs={{0,9},{1,0},{2,1},{3,2},{4,3},{5,4},{6,5},{7,6},{38,7},{39,38},{36... | collective-permute-start | bytes 774152 | tf_op jit(solution)/shard_map/ppermute | solution.py:432
  48.5 4.2 %collective-permute-start.7 = (bf16[16,896]{1,0:T(8,128)(2,1)S(1)}, bf16[16,896]{1,0:T(8,128)(2,1)S(1)}, u32[]{:S(2)}, u32[]{:S(2)}) collective-permute-start(bf16[16,896]{1,0:T(8,128)(2,1)S(1)} %get-tuple-element.174), channel_id=1, source_target_pairs={{0,8},{1,9},{2,0},{3,1},{4,2},{5,3},{6,4},{7,5},{38,6},{39,7},{36,... | collective-permute-start | bytes 86024 | tf_op jit(solution)/shard_map/ppermute | solution.py:432
  52.0 16.8 %copy-start = (bf16[1024,768]{1,0:T(8,128)(2,1)S(1)}, bf16[1024,768]{1,0:T(8,128)(2,1)}, u32[]{:S(2)}) copy-start(bf16[1024,768]{1,0:T(8,128)(2,1)} %emb_ref.1) | copy-start | bytes 4718596
  52.0 16.8 %copy-start.1 = (s32[1024]{0:T(1024)S(1)}, s32[1024]{0:T(1024)}, u32[]{:S(2)}) copy-start(s32[1024]{0:T(1024)} %param.12) | copy-start | bytes 12292
  52.0 16.8 %copy-start.2 = (s32[1024]{0:T(1024)S(1)}, s32[1024]{0:T(1024)}, u32[]{:S(2)}) copy-start(s32[1024]{0:T(1024)} %param.13) | copy-start | bytes 12292
  69.0 0.6 copy-start.3

commit v6 on v5

--- a/solution.py
+++ b/solution.py
@@ -210,9 +210,8 @@
         jnp.sum(jnp.clip(queue - SLOTS, 0.0, float(SLOTS)), axis=0, keepdims=True) - FAR
     )
     over_long = jnp.max(queue, axis=0, keepdims=True) - 2.0 * SLOTS
-    bad_ref[0, 0] = (
-        jnp.max(jnp.maximum(jnp.maximum(over_near, over_far), over_long)) > 0.0
-    ).astype(I32)
+    worst = jnp.maximum(jnp.maximum(over_near, over_far), over_long)
+    bad_ref[...] = jnp.where(jnp.max(worst, axis=1, keepdims=True) > 0.0, 1, 0)
 
     lane = iota((N, N), 1)
     hops = pltpu.roll(meta, N - 16, 1)
@@ -267,8 +266,6 @@
             jax.ShapeDtypeStruct((FAR, D + META), BF16),
             jax.ShapeDtypeStruct((1, 1), I32),
         ),
-        out_specs=(pl.BlockSpec(memory_space=pltpu.VMEM),) * 4
-        + (pl.BlockSpec(memory_space=pltpu.SMEM),),
         scratch_shapes=[pltpu.VMEM((MAIN, 128), F32), pltpu.VMEM((MAIN, 128), F32)],
         compiler_params=LIMIT,
         name="unpack",

time: 69.8 us -> 69.7 us (level)
  no operation moved by 1% of the time
where the time goes in v6:
time: 69.7 us; the launch traced here: 69.6 us
  blocking collectives  55.4 us (79%)
  Pallas kernels  10.7 us (15%)
  starting transfers between devices  0.94 us (1%)
  waiting for transfers between devices  0.89 us (1%)
  between operations  0.87 us (1%)
    all_to_all x2, blocking collectives, swapped(): return lax.all_to_all(array, 'dev', split_axis=0, concat_axis=0, tiled=True)  55.4 us
    pallas_call x1, Pallas kernels, pack(): pl.pallas_call(pack_kernel, in_specs=[pl.BlockSpec(memory_space=pl.ANY)]...  4.13 us
    pallas_call x1, Pallas kernels, local_best(): pl.pallas_call(local_kernel, out_shape=(jax.ShapeDtypeStruct((16, ALL), F...  3.42 us
    pallas_call x1, Pallas kernels, unpack(): pl.pallas_call(unpack_kernel, out_shape=(jax.ShapeDtypeStruct((EXTRA, D),...  1.6 us
  transfers between devices with their start and end apart: 2, of which 1 were waited for; matrix products, arithmetic and copies ran while one was open for 0% of the time, Pallas kernels for 5%

profile of v6, /device:TPU:1, one launch (start us, length us, event | category | flops | bytes accessed | tf_op | source)
XLA Modules:
  0.0 69.6 jit_solution(10761288168654795952)
XLA Ops:
  0.0 4.1 %pack.1 = (bf16[1024,1024]{1,0:T(8,128)(2,1)S(1)}, s32[2,1024]{1,0:T(2,128)S(1)}) custom-call(bf16[1024,768]{1,0:T(8,128)(2,1)} %emb_ref.1, s32[1,1024]{1,0:T(1,128)} %bitcast.101, s32[1,1024]{1,0:T(1,128)} %bitcast.102), custom_call_target="tpu_custom_call" | custom-call | tf_op jit(solution)/shard_map/pack/pallas_call | solution.py:175
  4.1 41.8 %all_to_all.45 = bf16[128,8,1024]{2,1,0:T(8,128)(2,1)S(1)} all-to-all(bf16[128,8,1024]{2,1,0:T(8,128)(2,1)S(1)} %bitcast.84), channel_id=1, replica_groups=mesh['dev'=128] {'dev'}, dimensions={0} | all-to-all | bytes 4194304 | tf_op jit(solution)/shard_map/all_to_all | solution.py:433
  46.0 1.6 %unpack.1 = (bf16[256,768]{1,0:T(8,128)(2,1)S(1)}, f32[128,128]{1,0:T(8,128)S(1)}, bf16[144,896]{1,0:T(8,128)(2,1)S(1)}, bf16[16,896]{1,0:T(8,128)(2,1)S(1)}, s32[1,1]{1,0:T(1,128)}) custom-call(bf16[1024,1024]{1,0:T(8,128)(2,1)S(1)} %bitcast.81), custom_call_target="tpu_custom_call" | custom-call | tf_op jit(solution)/shard_map/unpack/pallas_call | solution.py:260
  47.6 0.9 %collective-permute-start.6 = (bf16[144,896]{1,0:T(8,128)(2,1)S(1)}, bf16[144,896]{1,0:T(8,128)(2,1)S(1)}, u32[]{:S(2)}, u32[]{:S(2)}) collective-permute-start(bf16[144,896]{1,0:T(8,128)(2,1)S(1)} %get-tuple-element.173), channel_id=1, source_target_pairs={{0,9},{1,0},{2,1},{3,2},{4,3},{5,4},{6,5},{7,6},{38,7},{39,38},{36... | collective-permute-start | bytes 774152 | tf_op jit(solution)/shard_map/ppermute | solution.py:429
  48.5 0.0 collective-permute-start.7
  48.5 3.4 %local_best.1 = (f32[16,1280]{1,0:T(8,128)S(1)}, f32[8,1280]{1,0:T(8,128)S(1)}) custom-call(bf16[1024,1024]{1,0:T(8,128)(2,1)S(1)} %bitcast.82, bf16[256,768]{1,0:T(8,128)(2,1)S(1)} %get-tuple-element.165.late_ref, f32[128,128]{1,0:T(8,128)S(1)} %get-tuple-element.166.meta_ref), custom_call_target="tpu_custom_call" | custom-call | flops 2516582400 | bytes 3932160 | tf_op jit(solution)/shard_map/local_best/pallas_call | solution.py:319
  51.9 0.0 copy-start
  51.9 0.0 copy-start.1
  51.9 0.0 copy-start.2
  52.7 0.0 collective-permute-done.7.far_ref
  52.7 0.9 %collective-permute-done.6.near_ref = bf16[144,896]{1,0:T(8,128)(2,1)S(1)} collective-permute-done((bf16[144,896]{1,0:T(8,128)(2,1)S(1)}, bf16[144,896]{1,0:T(8,128)(2,1)S(1)}, u32[]{:S(2)}, u32[]{:S(2)}) %collective-permute-start.6) | collective-permute-done | bytes 258080 | tf_op jit(solution)/shard_map/ppermute | solution.py:429
  53.6 1.2 %cross_best.1 = f32[128,128]{1,0:T(8,128)S(1)} custom-call(bf16[1024,1024]{1,0:T(8,128)(2,1)S(1)} %bitcast.83, bf16[256,768]{1,0:T(8,128)(2,1)S(1)} %get-tuple-element.165.late_ref, f32[16,1280]{1,0:T(8,128)S(1)} %get-tuple-element.171.row_ref, f32[8,1280]{1,0:T(8,128)S(1)} %get-tuple-element.172.best_ref, ...), custom_call_target="tpu_custom_call" | custom-call | tf_op jit(solution)/shard_map/cross_best/pallas_call | solution.py:395
  54.8 13.6 %all_to_all.46 = f32[128,1,128]{2,1,0:T(1,128)S(1)} all-to-all(f32[128,1,128]{2,1,0:T(1,128)S(1)} %bitcast.85), channel_id=1, replica_groups=mesh['dev'=128] {'dev'}, dimensions={0} | all-to-all | bytes 131072 | tf_op jit(solution)/shard_map/all_to_all | solution.py:433
  68.4 0.3 pick.1
  68.7 0.0 copy-done
  68.7 0.0 copy-done.1
  68.7 0.0 copy-done.2
  68.7 0.2 conditional.1
  69.0 0.0 copy-start.3
  69.0 0.6 copy-done.3
Async XLA Ops:
  47.6 6.1 %collective-permute-start.6 = (bf16[144,896]{1,0:T(8,128)(2,1)S(1)}, bf16[144,896]{1,0:T(8,128)(2,1)S(1)}, u32[]{:S(2)}, u32[]{:S(2)}) collective-permute-start(bf16[144,896]{1,0:T(8,128)(2,1)S(1)} %get-tuple-element.173), channel_id=1, source_target_pairs={{0,9},{1,0},{2,1},{3,2},{4,3},{5,4},{6,5},{7,6},{38,7},{39,38},{36... | collective-permute-start | bytes 774152 | tf_op jit(solution)/shard_map/ppermute | solution.py:429
  48.5 4.2 %collective-permute-start.7 = (bf16[16,896]{1,0:T(8,128)(2,1)S(1)}, bf16[16,896]{1,0:T(8,128)(2,1)S(1)}, u32[]{:S(2)}, u32[]{:S(2)}) collective-permute-start(bf16[16,896]{1,0:T(8,128)(2,1)S(1)} %get-tuple-element.174), channel_id=1, source_target_pairs={{0,8},{1,9},{2,0},{3,1},{4,2},{5,3},{6,4},{7,5},{38,6},{39,7},{36,... | collective-permute-start | bytes 86024 | tf_op jit(solution)/shard_map/ppermute | solution.py:429
  51.9 16.8 %copy-start = (bf16[1024,768]{1,0:T(8,128)(2,1)S(1)}, bf16[1024,768]{1,0:T(8,128)(2,1)}, u32[]{:S(2)}) copy-start(bf16[1024,768]{1,0:T(8,128)(2,1)} %emb_ref.1) | copy-start | bytes 4718596
  51.9 16.8 %copy-start.1 = (s32[1024]{0:T(1024)S(1)}, s32[1024]{0:T(1024)}, u32[]{:S(2)}) copy-start(s32[1024]{0:T(1024)} %param.12) | copy-start | bytes 12292
  51.9 16.8 %copy-start.2 = (s32[1024]{0:T(1024)S(1)}, s32[1024]{0:T(1024)}, u32[]{:S(2)}) copy-start(s32[1024]{0:T(1024)} %param.13) | copy-start | bytes 12292
  69.0 0.6 copy-start.3

commit v7 on v5

--- a/solution.py
+++ b/solution.py
@@ -295,27 +295,27 @@
         own[...],
         jnp.concatenate([weights(RANK, (N, N), 0), weights(CLUSTER, (N, N), 0)], axis=1),
     )
-    best_ref[...] = jnp.full((8, ALL), -1.0, F32)
-
     def rows_of(b):
         if b * 256 < MAIN:
             return got_ref[b * 256 : (b + 1) * 256, :D]
         return late_ref[...]
 
-    blocks = ALL // 256
-    for i in range(blocks):
-        rank = column[i * 256 : (i + 1) * 256, :128]
-        cluster = column[i * 256 : (i + 1) * 256, 128:]
-        rank = jnp.concatenate([rank, rank], axis=1)
-        cluster = jnp.concatenate([cluster, cluster], axis=1)
-        for j in range(blocks):
-            across = slice(j * 256, (j + 1) * 256)
-            similar = dot_nt(rows_of(i), rows_of(j))
-            earlier = (cluster == row_ref[8:9, across]) & (rank < row_ref[0:1, across])
-            kept = jnp.where(earlier, similar, -1.0)
-            best_ref[:, across] = jnp.maximum(
-                best_ref[:, across], jnp.max(kept.reshape(32, 8, 256), axis=0)
-            )
+    for j in range(ALL // 256):
+        across = slice(j * 256, (j + 1) * 256)
+        held = rows_of(j)
+        best = jnp.full((8, 256), -1.0, F32)
+        for first, rows in ((0, got_ref[:, :D]), (MAIN, late_ref[...])):
+            similar = dot_nt(rows, held)
+            for i in range(rows.shape[0] // 256):
+                at = slice(first + i * 256, first + (i + 1) * 256)
+                rank = column[at, :128]
+                cluster = column[at, 128:]
+                rank = jnp.concatenate([rank, rank], axis=1)
+                cluster = jnp.concatenate([cluster, cluster], axis=1)
+                earlier = (cluster == row_ref[8:9, across]) & (rank < row_ref[0:1, across])
+                kept = jnp.where(earlier, similar[i * 256 : (i + 1) * 256], -1.0)
+                best = jnp.maximum(best, jnp.max(kept.reshape(32, 8, 256), axis=0))
+        best_ref[:, across] = best
 
 
 def local_best(got, late, meta):

time: 69.8 us -> 69.8 us (level)
  no operation moved by 1% of the time
where the time goes in v7:
time: 69.8 us; the launch traced here: 69.6 us
  blocking collectives  55.4 us (79%)
  Pallas kernels  10.5 us (15%)
  starting transfers between devices  1 us (1%)
  waiting for transfers between devices  0.99 us (1%)
  between operations  0.87 us (1%)
    all_to_all x2, blocking collectives, swapped(): return lax.all_to_all(array, 'dev', split_axis=0, concat_axis=0, tiled=True)  55.4 us
    pallas_call x1, Pallas kernels, pack(): pl.pallas_call(pack_kernel, in_specs=[pl.BlockSpec(memory_space=pl.ANY)]...  4.13 us
    pallas_call x1, Pallas kernels, local_best(): pl.pallas_call(local_kernel, out_shape=(jax.ShapeDtypeStruct((16, ALL), F...  3.33 us
    pallas_call x1, Pallas kernels, unpack(): pl.pallas_call(unpack_kernel, out_shape=(jax.ShapeDtypeStruct((EXTRA, D),...  1.56 us
  transfers between devices with their start and end apart: 2, of which 1 were waited for; matrix products, arithmetic and copies ran while one was open for 0% of the time, Pallas kernels for 5%

profile of v7, /device:TPU:1, one launch (start us, length us, event | category | flops | bytes accessed | tf_op | source)
XLA Modules:
  0.0 69.6 jit_solution(2001718043150358136)
XLA Ops:
  0.0 4.1 %pack.1 = (bf16[1024,1024]{1,0:T(8,128)(2,1)S(1)}, s32[2,1024]{1,0:T(2,128)S(1)}) custom-call(bf16[1024,768]{1,0:T(8,128)(2,1)} %emb_ref.1, s32[1,1024]{1,0:T(1,128)} %bitcast.101, s32[1,1024]{1,0:T(1,128)} %bitcast.102), custom_call_target="tpu_custom_call" | custom-call | tf_op jit(solution)/shard_map/pack/pallas_call | solution.py:175
  4.1 41.8 %all_to_all.45 = bf16[128,8,1024]{2,1,0:T(8,128)(2,1)S(1)} all-to-all(bf16[128,8,1024]{2,1,0:T(8,128)(2,1)S(1)} %bitcast.84), channel_id=1, replica_groups=mesh['dev'=128] {'dev'}, dimensions={0} | all-to-all | bytes 4194304 | tf_op jit(solution)/shard_map/all_to_all | solution.py:436
  46.0 1.6 %unpack.1 = (bf16[256,768]{1,0:T(8,128)(2,1)S(1)}, f32[128,128]{1,0:T(8,128)S(1)}, bf16[144,896]{1,0:T(8,128)(2,1)S(1)}, bf16[16,896]{1,0:T(8,128)(2,1)S(1)}, s32[1,1]{1,0:T(1,128)}) custom-call(bf16[1024,1024]{1,0:T(8,128)(2,1)S(1)} %bitcast.81), custom_call_target="tpu_custom_call" | custom-call | tf_op jit(solution)/shard_map/unpack/pallas_call | solution.py:261
  47.5 1.0 %collective-permute-start.6 = (bf16[144,896]{1,0:T(8,128)(2,1)S(1)}, bf16[144,896]{1,0:T(8,128)(2,1)S(1)}, u32[]{:S(2)}, u32[]{:S(2)}) collective-permute-start(bf16[144,896]{1,0:T(8,128)(2,1)S(1)} %get-tuple-element.173), channel_id=1, source_target_pairs={{0,9},{1,0},{2,1},{3,2},{4,3},{5,4},{6,5},{7,6},{38,7},{39,38},{36... | collective-permute-start | bytes 774152 | tf_op jit(solution)/shard_map/ppermute | solution.py:432
  48.5 0.0 collective-permute-start.7
  48.5 3.3 %local_best.1 = (f32[16,1280]{1,0:T(8,128)S(1)}, f32[8,1280]{1,0:T(8,128)S(1)}) custom-call(bf16[1024,1024]{1,0:T(8,128)(2,1)S(1)} %bitcast.82, bf16[256,768]{1,0:T(8,128)(2,1)S(1)} %get-tuple-element.165.late_ref, f32[128,128]{1,0:T(8,128)S(1)} %get-tuple-element.166.meta_ref), custom_call_target="tpu_custom_call" | custom-call | flops 2516582400 | bytes 3932160 | tf_op jit(solution)/shard_map/local_best/pallas_call | solution.py:322
  51.9 0.0 copy-start
  51.9 0.0 copy-start.1
  51.9 0.0 copy-start.2
  52.7 0.0 collective-permute-done.7.far_ref
  52.7 1.0 %collective-permute-done.6.near_ref = bf16[144,896]{1,0:T(8,128)(2,1)S(1)} collective-permute-done((bf16[144,896]{1,0:T(8,128)(2,1)S(1)}, bf16[144,896]{1,0:T(8,128)(2,1)S(1)}, u32[]{:S(2)}, u32[]{:S(2)}) %collective-permute-start.6) | collective-permute-done | bytes 258080 | tf_op jit(solution)/shard_map/ppermute | solution.py:432
  53.7 1.2 %cross_best.1 = f32[128,128]{1,0:T(8,128)S(1)} custom-call(bf16[1024,1024]{1,0:T(8,128)(2,1)S(1)} %bitcast.83, bf16[256,768]{1,0:T(8,128)(2,1)S(1)} %get-tuple-element.165.late_ref, f32[16,1280]{1,0:T(8,128)S(1)} %get-tuple-element.171.row_ref, f32[8,1280]{1,0:T(8,128)S(1)} %get-tuple-element.172.best_ref, ...), custom_call_target="tpu_custom_call" | custom-call | tf_op jit(solution)/shard_map/cross_best/pallas_call | solution.py:398
  54.9 13.6 %all_to_all.46 = f32[128,1,128]{2,1,0:T(1,128)S(1)} all-to-all(f32[128,1,128]{2,1,0:T(1,128)S(1)} %bitcast.85), channel_id=1, replica_groups=mesh['dev'=128] {'dev'}, dimensions={0} | all-to-all | bytes 131072 | tf_op jit(solution)/shard_map/all_to_all | solution.py:436
  68.4 0.3 pick.1
  68.7 0.0 copy-done
  68.7 0.0 copy-done.1
  68.8 0.0 copy-done.2
  68.8 0.2 conditional.1
  69.0 0.0 copy-start.3
  69.0 0.6 copy-done.3
Async XLA Ops:
  47.5 6.1 %collective-permute-start.6 = (bf16[144,896]{1,0:T(8,128)(2,1)S(1)}, bf16[144,896]{1,0:T(8,128)(2,1)S(1)}, u32[]{:S(2)}, u32[]{:S(2)}) collective-permute-start(bf16[144,896]{1,0:T(8,128)(2,1)S(1)} %get-tuple-element.173), channel_id=1, source_target_pairs={{0,9},{1,0},{2,1},{3,2},{4,3},{5,4},{6,5},{7,6},{38,7},{39,38},{36... | collective-permute-start | bytes 774152 | tf_op jit(solution)/shard_map/ppermute | solution.py:432
  48.5 4.1 %collective-permute-start.7 = (bf16[16,896]{1,0:T(8,128)(2,1)S(1)}, bf16[16,896]{1,0:T(8,128)(2,1)S(1)}, u32[]{:S(2)}, u32[]{:S(2)}) collective-permute-start(bf16[16,896]{1,0:T(8,128)(2,1)S(1)} %get-tuple-element.174), channel_id=1, source_target_pairs={{0,8},{1,9},{2,0},{3,1},{4,2},{5,3},{6,4},{7,5},{38,6},{39,7},{36,... | collective-permute-start | bytes 86024 | tf_op jit(solution)/shard_map/ppermute | solution.py:432
  51.9 16.9 %copy-start = (bf16[1024,768]{1,0:T(8,128)(2,1)S(1)}, bf16[1024,768]{1,0:T(8,128)(2,1)}, u32[]{:S(2)}) copy-start(bf16[1024,768]{1,0:T(8,128)(2,1)} %emb_ref.1) | copy-start | bytes 4718596
  51.9 16.9 %copy-start.1 = (s32[1024]{0:T(1024)S(1)}, s32[1024]{0:T(1024)}, u32[]{:S(2)}) copy-start(s32[1024]{0:T(1024)} %param.12) | copy-start | bytes 12292
  51.9 16.9 %copy-start.2 = (s32[1024]{0:T(1024)S(1)}, s32[1024]{0:T(1024)}, u32[]{:S(2)}) copy-start(s32[1024]{0:T(1024)} %param.13) | copy-start | bytes 12292
  69.0 0.6 copy-start.3
